TPU v7x, 512 devices: a whole 4x8x8 slice. The times are simulated.
512 devices in a mesh: rad: 32 (over x, y), ang: 16 (over z, core).
Axes of the slice: x: 4, y: 8, z: 8, core: 2. Of those that a mesh axis runs over, the one named last changes fastest.
Arguments:
- field: bfloat16 [512, 1024, 2048], P('rad', 'ang'), may hold values from -48 to 48
- start: float32 [512, 128], replicated, may hold values from -6 to 6
Outputs:
- core: bfloat16 [128, 1024, 2048], P(None, ('ang', 'rad'))
All inputs are finite; a program needn't handle non-finite values.
Results may differ from a plain program's by a relative error of at most 0.004.
The roundings to bfloat16 on the way count: a program that leaves them out, or rounds other values in their place, can miss the bound.
Values may be sent and summed in bfloat16 or wider, within the bound.
No kernel may reach another device: no remote copies, remote signals or barrier semaphores. Data moves between devices by JAX's collectives and lax.ppermute only.
A program may use at most 64 MiB of HBM per device.

v0:
```python
import jax
import jax.numpy as jnp
from jax import lax
from jax.sharding import PartitionSpec as P

ITERS = 2


def orthonormal(grown):
    inner = jnp.dot(grown.T, grown, precision=lax.Precision.HIGHEST)
    lower = jnp.linalg.cholesky(inner)
    return lax.linalg.triangular_solve(lower, grown, left_side=False, lower=True, transpose_a=True)


def subspace(gram, start):
    basis = start
    for step in range(ITERS):
        basis = orthonormal(jnp.dot(gram, basis, precision=lax.Precision.HIGHEST))
    return basis


def on_device(field, start):
    regrouped = lax.all_to_all(field, "rad", split_axis=1, concat_axis=0, tiled=True)
    radii, th_local, ph_local = regrouped.shape
    unfold = regrouped.reshape(radii, th_local * ph_local)
    partial_gram = jnp.einsum("ra,sa->rs", unfold, unfold, preferred_element_type=jnp.float32)
    gram = lax.psum(partial_gram, ("rad", "ang"))
    narrow = subspace(gram, start).astype(jnp.bfloat16)
    core = jnp.einsum("rk,ra->ka", narrow, unfold, preferred_element_type=jnp.float32)
    return core.astype(jnp.bfloat16).reshape(narrow.shape[1], th_local, ph_local)


def solution(mesh):
    return jax.shard_map(
        on_device,
        mesh=mesh,
        in_specs=(P("rad", "ang", None), P()),
        out_specs=P(None, ("ang", "rad"), None),
        check_vma=False,
    )
```

profile of v0, /device:TPU:1, one launch (start us, length us, event | category | flops | bytes accessed | tf_op | source)
XLA Modules:
  0.0 470.4 jit_solution(18080111519578669558)
XLA Ops:
  6.5 4.5 copy.8
  11.1 102.3 %all_to_all.15 = bf16[16,64,2048]{2,0,1:T(8,128)(2,1)S(1)} all-to-all(bf16[16,64,2048]{2,0,1:T(8,128)(2,1)S(1)} %copy.8), channel_id=1, replica_groups=mesh['rad'=32,'ang'=16] {'rad'}, dimensions={1} | all-to-all | bytes 8388608 | tf_op jit(solution)/shard_map/all_to_all | solution.py:23
  113.4 6.3 %copy.9 = bf16[16,32,2,2048]{3,2,0,1:T(2,128)(2,1)} copy(bf16[16,32,2,2048]{3,0,2,1:T(8,128)(2,1)S(1)} %bitcast.45) | data formatting | bytes 8388608 | tf_op jit(solution)/shard_map/all_to_all | solution.py:23
  119.7 4.6 copy.12
  124.3 1.9 copy-done.1
  126.2 3.3 fusion.9
  129.6 276.8 %all-reduce.2.cloned.1.call-done = f32[512,512]{1,0:T(8,128)} async-done(((f32[512,512]{1,0:T(8,128)}), f32[512,512]{1,0:T(8,128)}) %all-reduce.2.cloned.1.call-update) | async-done | bytes 1048592 | tf_op jit(solution)/shard_map/psum | solution.py:27
  406.3 2.2 fusion.10
  408.5 0.6 fusion.11
  409.1 0.1 copy.10
  409.2 11.9 %cholesky.44 = f32[128,128]{1,0:T(8,128)S(1)} custom-call(f32[128,128]{1,0:T(8,128)S(1)} %fusion.6), custom_call_target="Cholesky" | custom-call | tf_op jit(solution)/shard_map/jit(cholesky)/cholesky | solution.py:11
  421.2 0.6 compare_reduce_fusion.1
  421.8 0.7 fusion.1
  422.5 9.8 %custom-call.6 = f32[1,128,128]{1,2,0:T(8,128)S(1)} custom-call(f32[1,128,128]{2,1,0:T(8,128)S(1)} %fusion.1), custom_call_target="InvertDiagBlocksLowerTriangular" | custom-call | tf_op jit(solution)/shard_map/triangular_solve/custom-call.0 | solution.py:12
  432.3 0.4 convolution_bitcast_fusion.1
  432.7 2.2 fusion.12
  435.0 0.6 fusion.13
  435.7 11.7 %cholesky.55 = f32[128,128]{1,0:T(8,128)S(1)} custom-call(f32[128,128]{1,0:T(8,128)S(1)} %fusion.4), custom_call_target="Cholesky" | custom-call | tf_op jit(solution)/shard_map/jit(cholesky)/cholesky | solution.py:11
  447.4 0.6 compare_reduce_fusion
  448.1 0.7 fusion.2
  448.7 9.8 %custom-call.7 = f32[1,128,128]{1,2,0:T(8,128)S(1)} custom-call(f32[1,128,128]{2,1,0:T(8,128)S(1)} %fusion.2), custom_call_target="InvertDiagBlocksLowerTriangular" | custom-call | tf_op jit(solution)/shard_map/triangular_solve/custom-call.0 | solution.py:12
  458.5 0.4 fusion
  459.0 3.0 convolution_convert_fusion
  461.9 1.6 reshape.19
  (10 shorter events, 0.2 us)
Async XLA Ops:
  6.5 399.8 %copy-start = (f32[512,128]{1,0:T(8,128)S(1)}, f32[512,128]{1,0:T(8,128)}, u32[]{:S(2)}) copy-start(f32[512,128]{1,0:T(8,128)} %param.6) | copy-start | bytes 786436
  6.5 399.8 %all-reduce.2.cloned.1.call-start = ((), (), s32[]{:S(2)}) async-start(), calls=%async_computation.1 | async-start | bytes 2097152 | tf_op jit(solution)/shard_map/psum | solution.py:27
  124.3 1.9 copy-start.1
Sparse Core Ops, SparseCore 0:
  129.7 276.5 all-reduce.1
where the time goes:
time: 471 us; the launch traced here: 470 us
  waiting for transfers between devices  277 us (59%)
  blocking collectives  102 us (22%)
  other arithmetic  45.9 us (10%)
  local copies, waits for them, and re-layouts  19.1 us (4%)
  between operations  13.5 us (3%)
  matrix products  12.7 us (3%)
    psum x1, waiting for transfers between devices, on_device(): gram = lax.psum(partial_gram, ('rad', 'ang'))  277 us
    all_to_all x1, blocking collectives, on_device(): lax.all_to_all(field, 'rad', split_axis=1, concat_axis=0, tiled=True)  102 us
    another operation x6, other arithmetic, orthonormal(): lower = jnp.linalg.cholesky(inner)  25 us
    another operation x4, other arithmetic, orthonormal(): lax.linalg.triangular_solve(lower, grown, left_side=False, lower=True, tr...  20.9 us
    unnamed x6, local copies, waits for them, and re-layouts  11 us
  transfers between devices with their start and end apart: 1, of which 1 were waited for; matrix products, arithmetic and copies ran while one was open for 0% of the time, Pallas kernels for 0%

commit v1 on v0

v1 whole, which is shorter than its diff:
```python
import functools

import jax
import jax.numpy as jnp
from jax import lax
from jax.experimental import pallas as pl
from jax.experimental.pallas import tpu as pltpu
from jax.sharding import Mesh, PartitionSpec as P

ITERS = 2
SUB = 8
TILE = 128
AXES = ("x", "y", "z", "core")
SIZES = (4, 8, 8, 2)
RAD = ("x", "y")
WIDE = ("x", "z")
MID = ("y", "core")
VMEM_LIMIT = 48 * 2**20


def group(names):
    size = 1
    for name in names:
        size *= SIZES[AXES.index(name)]
    return size


def pairs(parts):
    return [(i, j) for i in range(parts) for j in range(i, parts)]


def gram_kernel(u_ref, out_ref, acc_ref):
    step = pl.program_id(0) * pl.num_programs(1) + pl.program_id(1)
    last = pl.num_programs(0) * pl.num_programs(1) - 1
    src, _, radii, cells = u_ref.shape
    u = u_ref[...].reshape(src * radii, cells)
    half = src * radii // 2

    def outer(a, b):
        return lax.dot_general(a, b, (((1,), (1,)), ((), ())), preferred_element_type=jnp.float32)

    top = outer(u[:half], u)
    low = outer(u[half:], u[half:])

    @pl.when(step == 0)
    def _():
        acc_ref[:half] = top
        acc_ref[half:, half:] = low

    @pl.when(step > 0)
    def _():
        acc_ref[:half] += top
        acc_ref[half:, half:] += low

    @pl.when(step == last)
    def _():
        for n, (i, j) in enumerate(pairs(src * radii // TILE)):
            out_ref[n] = acc_ref[TILE * i:TILE * (i + 1), TILE * j:TILE * (j + 1)]


def partial_gram(regrouped):
    src, th, radii, ph = regrouped.shape
    order = src * radii
    cells = 1024
    count = len(pairs(order // TILE))
    return pl.pallas_call(
        gram_kernel,
        grid=(th, ph // cells),
        in_specs=[pl.BlockSpec((src, 1, radii, cells), lambda t, c: (0, t, 0, c))],
        out_specs=pl.BlockSpec((count, TILE, TILE), lambda t, c: (0, 0, 0)),
        out_shape=jax.ShapeDtypeStruct((count, TILE, TILE), jnp.float32),
        scratch_shapes=[pltpu.VMEM((order, order), jnp.float32)],
        compiler_params=pltpu.CompilerParams(vmem_limit_bytes=VMEM_LIMIT),
        cost_estimate=pl.CostEstimate(flops=2 * order * order * th * ph, bytes_accessed=2 * order * th * ph, transcendentals=0),
        name="gram",
    )(regrouped)


def sum_kernel(x_ref, out_ref):
    total = x_ref[0]
    for n in range(1, x_ref.shape[0]):
        total = total + x_ref[n]
    out_ref[...] = jnp.broadcast_to(total[None], out_ref.shape)


def sum_and_repeat(x, copies):
    return pl.pallas_call(
        sum_kernel,
        in_specs=[pl.BlockSpec(memory_space=pltpu.VMEM)],
        out_specs=pl.BlockSpec(memory_space=pltpu.VMEM),
        out_shape=jax.ShapeDtypeStruct((copies,) + x.shape[1:], jnp.float32),
        name="total",
    )(x)


def swap(x, names):
    return lax.all_to_all(x, names, split_axis=0, concat_axis=0, tiled=True)


def sum_everywhere(blocks):
    wide, mid = group(WIDE), group(MID)
    pieces = blocks.reshape(wide, -1, TILE)
    share = sum_and_repeat(swap(pieces, WIDE), mid)
    share = sum_and_repeat(swap(share, MID), wide)
    return swap(share, WIDE).reshape(blocks.shape)


def inverse_lower(inner):
    n = inner.shape[0]
    parts = n // SUB
    row = lax.broadcasted_iota(jnp.int32, (SUB, n), 0)
    col = lax.broadcasted_iota(jnp.int32, (SUB, n), 1)
    left = [inner[SUB * q:SUB * (q + 1)] for q in range(parts)]
    right = [jnp.where(col == row + SUB * q, 1.0, 0.0) for q in range(parts)]

    def spread(x, c):
        return jnp.broadcast_to(x[:, c:c + 1], (SUB, n))

    def pick(x, r):
        return jnp.broadcast_to(x[r:r + 1], (SUB, n))

    for p in range(parts):
        columns = {q: [spread(left[q], SUB * p + j) for j in range(SUB)] for q in range(p, parts)}
        pivots = jnp.ones((SUB, n), jnp.float32)
        for j in range(SUB):
            own = columns[p]
            pivot = pick(own[j], j)
            inv = 1.0 / pivot
            pivots = jnp.where(row == j, pivot, pivots)
            lead_left = pick(left[p], j)
            lead_right = pick(right[p], j)
            lead = [pick(own[c], j) for c in range(j + 1, SUB)]
            for q in range(p, parts):
                times = columns[q][j] * inv
                if q == p:
                    times = jnp.where(row > j, times, 0.0)
                left[q] = left[q] - times * lead_left
                right[q] = right[q] - times * lead_right
                for c in range(j + 1, SUB):
                    columns[q][c] = columns[q][c] - times * lead[c - j - 1]
        right[p] = right[p] / jnp.sqrt(pivots)
    return jnp.concatenate(right, axis=0)


def exact(a, b, dims):
    return lax.dot_general(
        a, b, ((dims[:1], dims[1:]), ((), ())),
        precision=lax.Precision.HIGHEST, preferred_element_type=jnp.float32,
    )


def core_kernel(blocks_ref, start_ref, u_ref, out_ref, gram_ref, basis_ref, held_ref, sem):
    copy = pltpu.make_async_copy(u_ref, held_ref, sem)
    copy.start()
    order = start_ref.shape[0]
    for n, (i, j) in enumerate(pairs(order // TILE)):
        block = blocks_ref[n]
        gram_ref[TILE * i:TILE * (i + 1), TILE * j:TILE * (j + 1)] = block
        if i != j:
            gram_ref[TILE * j:TILE * (j + 1), TILE * i:TILE * (i + 1)] = block.T
    basis_ref[...] = start_ref[...]

    def step(_, carry):
        grown = exact(gram_ref[...], basis_ref[...], (1, 0))
        inner = exact(grown, grown, (0, 0))
        basis_ref[...] = exact(grown, inverse_lower(inner), (1, 1))
        return carry

    lax.fori_loop(0, ITERS, step, 0)
    narrow = basis_ref[...].astype(jnp.bfloat16)
    copy.wait()
    src, th, radii, ph = held_ref.shape
    cells = 512
    for t in range(th):
        for c in range(ph // cells):
            u = held_ref[:, t, :, cells * c:cells * (c + 1)].reshape(src * radii, cells)
            core = lax.dot_general(narrow, u, (((0,), (0,)), ((), ())), preferred_element_type=jnp.float32)
            out_ref[:, t * ph + cells * c:t * ph + cells * (c + 1)] = core.astype(jnp.bfloat16)


def core_of(blocks, start, regrouped):
    order, rank = start.shape
    src, th, radii, ph = regrouped.shape
    vmem = pl.BlockSpec(memory_space=pltpu.VMEM)
    return pl.pallas_call(
        core_kernel,
        in_specs=[vmem, vmem, pl.BlockSpec(memory_space=pl.ANY)],
        out_specs=vmem,
        out_shape=jax.ShapeDtypeStruct((rank, th * ph), jnp.bfloat16),
        scratch_shapes=[
            pltpu.VMEM((order, order), jnp.float32),
            pltpu.VMEM((order, rank), jnp.float32),
            pltpu.VMEM(regrouped.shape, jnp.bfloat16),
            pltpu.SemaphoreType.DMA,
        ],
        compiler_params=pltpu.CompilerParams(vmem_limit_bytes=VMEM_LIMIT),
        name="subspace_and_core",
    )(blocks, start, regrouped)


def on_device(field, start):
    radii, th, ph = field.shape
    owners = group(RAD)
    sent = field.transpose(1, 0, 2).reshape(owners, th // owners, radii, ph)
    regrouped = swap(sent, RAD)
    blocks = sum_everywhere(partial_gram(regrouped))
    core = core_of(blocks, start, regrouped)
    return core.reshape(start.shape[1], th // owners, ph)


def solution(mesh):
    fine = Mesh(mesh.devices.reshape(SIZES), AXES)
    return jax.shard_map(
        on_device,
        mesh=fine,
        in_specs=(P(RAD, ("z", "core"), None), P()),
        out_specs=P(None, ("z", "core") + RAD, None),
        check_vma=False,
    )
```

time: 471 us -> 211 us (0.45)
  waiting for transfers between devices: 277 us -> 0 us
  blocking collectives: 102 us -> 180 us
  other arithmetic: 45.9 us -> 0 us
  Pallas kernels: 0 us -> 21.1 us
  between operations: 13.5 us -> 0.03 us
  matrix products: 12.7 us -> 0 us
  local copies, waits for them, and re-layouts: 19.1 us -> 10.2 us
    psum x1 -> x0, waiting for transfers between devices: 277 us -> none  [on_device(): gram = lax.psum(partial_gram, ('rad', 'ang'))]
    all_to_all x1 -> x4, blocking collectives: 102 us -> 180 us  [swap(): return lax.all_to_all(x, names, split_axis=0, concat_axis=0, tiled=True)]
    another operation x10 -> x0, other arithmetic: 45.9 us -> none  [the longest x6 25 us: orthonormal(): lower = jnp.linalg.cholesky(inner)]
    pallas_call x0 -> x4, Pallas kernels: none -> 21.1 us  [the longest x1 14.2 us: core_of(): pl.pallas_call(core_kernel, in_specs=[vmem, vmem, pl.BlockSpec(memory_spa...]
    dot_general x6 -> x0, matrix products: 11.9 us -> none  [the longest x2 4.43 us: subspace(): basis = orthonormal(jnp.dot(gram, basis, precision=lax.Precision.HIGHEST))]
    unnamed x6, local copies, waits for them, and re-layouts: 11 us -> 4.12 us
    all_to_all x1 -> x0, local copies, waits for them, and re-layouts: 6.29 us -> none  [on_device(): lax.all_to_all(field, 'rad', split_axis=1, concat_axis=0, tiled=True)]
  transfers between devices with their start and end apart: 1 -> 0, of which waited for: 1 -> 0; matrix products, arithmetic and copies ran while one was open for 0% -> 0% of each run, Pallas kernels for 0% -> 0%
where the time goes in v1:
time: 211 us
  blocking collectives  180 us (85%)
  Pallas kernels  21.1 us (10%)
  local copies, waits for them, and re-layouts  10.2 us (5%)
    all_to_all x4, blocking collectives, swap(): return lax.all_to_all(x, names, split_axis=0, concat_axis=0, tiled=True)  180 us
    pallas_call x1, Pallas kernels, core_of(): pl.pallas_call(core_kernel, in_specs=[vmem, vmem, pl.BlockSpec(memory_spa...  14.2 us
    transpose x1, local copies, waits for them, and re-layouts, on_device(): sent = field.transpose(1, 0, 2).reshape(owners, th // owners, radii, ph)  4.49 us

profile of v1, /device:TPU:1, one launch (start us, length us, event | category | flops | bytes accessed | tf_op | source)
XLA Modules:
  0.0 210.9 jit_solution(13846731894310456797)
XLA Ops:
  0.0 4.5 %copy.3 = bf16[64,16,2048]{2,1,0:T(8,128)(2,1)S(1)} copy(bf16[64,16,2048]{2,0,1:T(8,128)(2,1)} %bitcast.7) | data formatting | bytes 8388608 | tf_op jit(solution)/shard_map/transpose | solution.py:204
  4.5 102.3 %all_to_all.20.u_ref = bf16[32,2,16,2048]{3,2,1,0:T(8,128)(2,1)S(1)} all-to-all(bf16[32,2,16,2048]{3,2,1,0:T(8,128)(2,1)S(1)} %bitcast.6), channel_id=1, replica_groups=mesh['x'=4,'y'=8,'z'=8,'core'=2] {'x','y'}, dimensions={0} | all-to-all | bytes 8388608 | tf_op jit(solution)/shard_map/all_to_all | solution.py:97
  106.8 3.1 %gram.1 = f32[10,128,128]{2,1,0:T(8,128)S(1)} custom-call(bf16[32,2,16,2048]{3,2,1,0:T(8,128)(2,1)S(1)} %all_to_all.20.u_ref), custom_call_target="tpu_custom_call" | custom-call | flops 2147483648 | bytes 4194304 | tf_op jit(solution)/shard_map/gram/pallas_call | solution.py:66
  110.0 0.0 copy-start
  110.0 1.9 copy-done
  111.9 0.0 copy-start.2
  111.9 25.8 %all_to_all.21.x_ref = f32[32,40,128]{2,1,0:T(8,128)} all-to-all(f32[32,40,128]{2,1,0:T(8,128)S(1)} %bitcast.5), channel_id=1, replica_groups=mesh['x'=4,'y'=8,'z'=8,'core'=2] {'x','z'}, dimensions={0} | all-to-all | bytes 1310720 | tf_op jit(solution)/shard_map/all_to_all | solution.py:97
  137.7 1.9 total.2
  139.5 27.4 %all_to_all.22.x_ref = f32[16,40,128]{2,1,0:T(8,128)} all-to-all(f32[16,40,128]{2,1,0:T(8,128)} %total.2), channel_id=1, replica_groups=mesh['x'=4,'y'=8,'z'=8,'core'=2] {'y','core'}, dimensions={0} | all-to-all | bytes 655360 | tf_op jit(solution)/shard_map/all_to_all | solution.py:97
  167.0 1.9 total.3
  168.8 24.0 %all_to_all.23 = f32[32,40,128]{2,1,0:T(8,128)S(1)} all-to-all(f32[32,40,128]{2,1,0:T(8,128)} %total.3), channel_id=1, replica_groups=mesh['x'=4,'y'=8,'z'=8,'core'=2] {'x','z'}, dimensions={0} | all-to-all | bytes 1310720 | tf_op jit(solution)/shard_map/all_to_all | solution.py:97
  192.8 0.0 copy-done.2
  192.9 0.0 copy-start.1
  192.9 2.2 %copy-done.1 = bf16[32,2,16,2048]{3,2,1,0:T(8,128)(2,1)S(1)} copy-done((bf16[32,2,16,2048]{3,2,1,0:T(8,128)(2,1)S(1)}, bf16[32,2,16,2048]{3,2,1,0:T(8,128)(2,1)}, u32[]{:S(2)}) %copy-start.1) | copy-done | bytes 4194328
  195.0 14.2 %subspace_and_core.1 = bf16[128,4096]{1,0:T(8,128)(2,1)S(1)} custom-call(f32[10,128,128]{2,1,0:T(8,128)S(1)} %bitcast.4, f32[512,128]{1,0:T(8,128)S(1)} %copy-done.2, bf16[32,2,16,2048]{3,2,1,0:T(8,128)(2,1)S(1)} %copy-done.1), custom_call_target="tpu_custom_call" | custom-call | tf_op jit(solution)/shard_map/subspace_and_core/pallas_call | solution.py:185
  209.3 1.6 reshape.15
Async XLA Ops:
  110.0 1.9 copy-start
  111.9 81.0 %copy-start.2 = (f32[512,128]{1,0:T(8,128)S(1)}, f32[512,128]{1,0:T(8,128)}, u32[]{:S(2)}) copy-start(f32[512,128]{1,0:T(8,128)} %start_ref.1) | copy-start | bytes 786436
  192.9 2.2 %copy-start.1 = (bf16[32,2,16,2048]{3,2,1,0:T(8,128)(2,1)S(1)}, bf16[32,2,16,2048]{3,2,1,0:T(8,128)(2,1)}, u32[]{:S(2)}) copy-start(bf16[32,2,16,2048]{3,2,1,0:T(8,128)(2,1)} %copy-done) | copy-start | bytes 12582916

commit v2 on v1

v2 whole, which is shorter than its diff:
```python
import jax
import jax.numpy as jnp
from jax import lax
from jax.experimental import pallas as pl
from jax.experimental.pallas import tpu as pltpu
from jax.sharding import Mesh, PartitionSpec as P

ITERS = 2
SUB = 8
TILE = 128
AXES = ("x", "y", "z", "core")
SIZES = (4, 8, 8, 2)
RAD = ("x", "y")
WIDE = ("x", "z")
MID = ("y",)
VMEM_LIMIT = 24 * 2**20


def group(names):
    size = 1
    for name in names:
        size *= SIZES[AXES.index(name)]
    return size


def halves():
    return (((0, 1), (0, 2), (0, 3)), (0, 1)), (((1, 2), (1, 3), (2, 3)), (2, 3))


def tile_iota():
    return (lax.broadcasted_iota(jnp.int32, (TILE, TILE), d) for d in (0, 1))


def gram_kernel(u_ref, keep_ref, send_ref, acc_ref):
    src, th, radii, ph = u_ref.shape
    order = src * radii
    half = order // 2
    cells = 1024
    for t in range(th):
        for c in range(ph // cells):
            u = u_ref[:, t, :, cells * c:cells * (c + 1)].reshape(order, cells)
            top = lax.dot_general(u[:half], u, (((1,), (1,)), ((), ())), preferred_element_type=jnp.float32)
            low = lax.dot_general(u[half:], u[half:], (((1,), (1,)), ((), ())), preferred_element_type=jnp.float32)
            if t == 0 and c == 0:
                acc_ref[:half] = top
                acc_ref[half:, half:] = low
            else:
                acc_ref[:half] += top
                acc_ref[half:, half:] += low
    row, col = tile_iota()

    def block(i, j):
        return acc_ref[TILE * i:TILE * (i + 1), TILE * j:TILE * (j + 1)]

    def pack(ref, part):
        offs, (first, second) = part
        for n, (i, j) in enumerate(offs):
            ref[TILE * n:TILE * (n + 1)] = block(i, j)
        under = block(first, first)
        ref[TILE * 3:TILE * 4] = jnp.where(row > col, under, block(second, second))
        diagonal = jnp.sum(jnp.where(row == col, under, 0.0), axis=0, keepdims=True)
        ref[TILE * 4:] = jnp.broadcast_to(diagonal, (ref.shape[0] - TILE * 4, TILE))

    core = lax.axis_index("core")
    for own in (0, 1):
        @pl.when(core == own)
        def _():
            pack(keep_ref, halves()[own])
            pack(send_ref, halves()[1 - own])


def partial_gram(regrouped):
    src, th, radii, ph = regrouped.shape
    order = src * radii
    vmem = pl.BlockSpec(memory_space=pltpu.VMEM)
    out = jax.ShapeDtypeStruct((4 * TILE + group(WIDE), TILE), jnp.float32)
    return pl.pallas_call(
        gram_kernel,
        in_specs=[vmem],
        out_specs=[vmem, vmem],
        out_shape=[out, out],
        scratch_shapes=[pltpu.VMEM((order, order), jnp.float32)],
        compiler_params=pltpu.CompilerParams(vmem_limit_bytes=VMEM_LIMIT),
        name="gram",
    )(regrouped)


def unpack_half(packed, part, gram_ref):
    offs, (first, second) = part
    row, col = tile_iota()

    def put(i, j, value):
        gram_ref[TILE * i:TILE * (i + 1), TILE * j:TILE * (j + 1)] = value

    for n, (i, j) in enumerate(offs):
        value = packed[TILE * n:TILE * (n + 1)]
        put(i, j, value)
        put(j, i, value.T)
    shared = packed[TILE * 3:TILE * 4]
    diagonal = jnp.broadcast_to(packed[TILE * 4:TILE * 4 + 1], (TILE, TILE))
    turned = shared.T
    put(first, first, jnp.where(row > col, shared, jnp.where(row < col, turned, diagonal)))
    put(second, second, jnp.where(row > col, turned, shared))


def swap(x, names):
    return lax.all_to_all(x, names, split_axis=0, concat_axis=0, tiled=True)


def swap_core(x):
    return lax.ppermute(x, "core", [(0, 1), (1, 0)])


def repeat(x, copies):
    return jnp.broadcast_to(x[None], (copies,) + x.shape)


def sum_everywhere(keep, send):
    half = keep + swap_core(send)
    share = jnp.sum(swap(half.reshape(group(WIDE), 1, -1), WIDE), axis=0)
    share = jnp.sum(swap(repeat(share, group(MID)), MID), axis=0)
    mine = swap(repeat(share, group(WIDE)), WIDE).reshape(half.shape)
    return mine, swap_core(mine)


def inverse_lower(inner):
    n = inner.shape[0]
    parts = n // SUB
    row = lax.broadcasted_iota(jnp.int32, (SUB, n), 0)
    col = lax.broadcasted_iota(jnp.int32, (SUB, n), 1)
    left = [inner[SUB * q:SUB * (q + 1)] for q in range(parts)]
    right = [jnp.where(col == row + SUB * q, 1.0, 0.0) for q in range(parts)]

    def spread(x, c):
        return jnp.broadcast_to(x[:, c:c + 1], (SUB, n))

    def pick(x, r):
        return jnp.broadcast_to(x[r:r + 1], (SUB, n))

    for p in range(parts):
        columns = {q: [spread(left[q], SUB * p + j) for j in range(SUB)] for q in range(p, parts)}
        pivots = jnp.ones((SUB, n), jnp.float32)
        for j in range(SUB):
            own = columns[p]
            pivot = pick(own[j], j)
            inv = 1.0 / pivot
            pivots = jnp.where(row == j, pivot, pivots)
            lead_left = pick(left[p], j)
            lead_right = pick(right[p], j)
            lead = [pick(own[c], j) for c in range(j + 1, SUB)]
            for q in range(p, parts):
                times = columns[q][j] * inv
                if q == p:
                    times = jnp.where(row > j, times, 0.0)
                left[q] = left[q] - times * lead_left
                right[q] = right[q] - times * lead_right
                for c in range(j + 1, SUB):
                    columns[q][c] = columns[q][c] - times * lead[c - j - 1]
        right[p] = right[p] / jnp.sqrt(pivots)
    return jnp.concatenate(right, axis=0)


def exact(a, b, dims):
    return lax.dot_general(
        a, b, ((dims[:1], dims[1:]), ((), ())),
        precision=lax.Precision.HIGHEST, preferred_element_type=jnp.float32,
    )


def core_kernel(mine_ref, other_ref, start_ref, u_ref, out_ref, gram_ref, basis_ref):
    core = lax.axis_index("core")
    for own in (0, 1):
        @pl.when(core == own)
        def _():
            unpack_half(mine_ref[...], halves()[own], gram_ref)
            unpack_half(other_ref[...], halves()[1 - own], gram_ref)
    basis_ref[...] = start_ref[...]

    def step(_, carry):
        grown = exact(gram_ref[...], basis_ref[...], (1, 0))
        inner = exact(grown, grown, (0, 0))
        basis_ref[...] = exact(grown, inverse_lower(inner), (1, 1))
        return carry

    lax.fori_loop(0, ITERS, step, 0)
    narrow = basis_ref[...].T.astype(jnp.bfloat16)
    src, th, radii, ph = u_ref.shape
    cells = 512
    for t in range(th):
        for c in range(ph // cells):
            u = u_ref[:, t, :, cells * c:cells * (c + 1)].reshape(src * radii, cells)
            core = jnp.dot(narrow, u, preferred_element_type=jnp.float32)
            out_ref[:, t * ph + cells * c:t * ph + cells * (c + 1)] = core.astype(jnp.bfloat16)


def core_of(mine, other, start, regrouped):
    order, rank = start.shape
    src, th, radii, ph = regrouped.shape
    vmem = pl.BlockSpec(memory_space=pltpu.VMEM)
    return pl.pallas_call(
        core_kernel,
        in_specs=[vmem] * 4,
        out_specs=vmem,
        out_shape=jax.ShapeDtypeStruct((rank, th * ph), jnp.bfloat16),
        scratch_shapes=[pltpu.VMEM((order, order), jnp.float32), pltpu.VMEM((order, rank), jnp.float32)],
        compiler_params=pltpu.CompilerParams(vmem_limit_bytes=VMEM_LIMIT),
        name="subspace_and_core",
    )(mine, other, start, regrouped)


def on_device(field, start):
    radii, th, ph = field.shape
    owners = group(RAD)
    sent = field.transpose(1, 0, 2).reshape(owners, th // owners, radii, ph)
    regrouped = swap(sent, RAD)
    mine, other = sum_everywhere(*partial_gram(regrouped))
    core = core_of(mine, other, start, regrouped)
    return core.reshape(start.shape[1], th // owners, ph)


def solution(mesh):
    fine = Mesh(mesh.devices.reshape(SIZES), AXES)
    return jax.shard_map(
        on_device,
        mesh=fine,
        in_specs=(P(RAD, ("z", "core"), None), P()),
        out_specs=P(None, ("z", "core") + RAD, None),
        check_vma=False,
    )
```

time: 211 us -> 194 us (0.919)
  blocking collectives: 180 us -> 150 us
  starting transfers between devices: 0 us -> 13.7 us
  Pallas kernels: 21.1 us -> 16 us
  waiting for transfers between devices: 0 us -> 2.33 us
    all_to_all x4, blocking collectives: 180 us -> 150 us  [swap(): return lax.all_to_all(x, names, split_axis=0, concat_axis=0, tiled=True)]
    ppermute x0 -> x2, starting transfers between devices: none -> 13.7 us  [swap_core(): return lax.ppermute(x, 'core', [(0, 1), (1, 0)])]
    pallas_call x4 -> x2, Pallas kernels: 21.1 us -> 16 us  [the longest x1 14.2 us: core_of(): pl.pallas_call(core_kernel, in_specs=[vmem] * 4, out_specs=vmem, out_shap...]
    ppermute x0 -> x2, waiting for transfers between devices: none -> 2.33 us  [swap_core(): return lax.ppermute(x, 'core', [(0, 1), (1, 0)])]
  transfers between devices with their start and end apart: 0 -> 2, of which waited for: 0 -> 2; matrix products, arithmetic and copies ran while one was open for 0% -> 0% of each run, Pallas kernels for 0% -> 0%
where the time goes in v2:
time: 194 us; the launch traced here: 193 us
  blocking collectives  150 us (77%)
  Pallas kernels  16 us (8%)
  starting transfers between devices  13.7 us (7%)
  local copies, waits for them, and re-layouts  10.4 us (5%)
  waiting for transfers between devices  2.33 us (1%)
    all_to_all x4, blocking collectives, swap(): return lax.all_to_all(x, names, split_axis=0, concat_axis=0, tiled=True)  150 us
    pallas_call x1, Pallas kernels, core_of(): pl.pallas_call(core_kernel, in_specs=[vmem] * 4, out_specs=vmem, out_shap...  14.2 us
    ppermute x2, starting transfers between devices, swap_core(): return lax.ppermute(x, 'core', [(0, 1), (1, 0)])  13.7 us
    transpose x1, local copies, waits for them, and re-layouts, on_device(): sent = field.transpose(1, 0, 2).reshape(owners, th // owners, radii, ph)  4.49 us
    unnamed x6, local copies, waits for them, and re-layouts  4.13 us
  transfers between devices with their start and end apart: 2, of which 2 were waited for; matrix products, arithmetic and copies ran while one was open for 0% of the time, Pallas kernels for 0%

profile of v2, /device:TPU:1, one launch (start us, length us, event | category | flops | bytes accessed | tf_op | source)
XLA Modules:
  0.0 193.3 jit_solution(17524579518710531200)
XLA Ops:
  0.0 4.5 %copy.8 = bf16[64,16,2048]{2,1,0:T(8,128)(2,1)S(1)} copy(bf16[64,16,2048]{2,0,1:T(8,128)(2,1)} %bitcast.7) | data formatting | bytes 8388608 | tf_op jit(solution)/shard_map/transpose | solution.py:214
  4.5 102.3 %all_to_all.20.u_ref = bf16[32,2,16,2048]{3,2,1,0:T(8,128)(2,1)S(1)} all-to-all(bf16[32,2,16,2048]{3,2,1,0:T(8,128)(2,1)S(1)} %bitcast.6), channel_id=1, replica_groups=mesh['x'=4,'y'=8,'z'=8,'core'=2] {'x','y'}, dimensions={0} | all-to-all | bytes 8388608 | tf_op jit(solution)/shard_map/all_to_all | solution.py:107
  106.8 0.0 copy-start.2
  106.8 1.9 gram.1
  108.7 0.0 copy-start
  108.7 1.9 copy-done
  110.7 6.9 %collective-permute-start = (f32[544,128]{1,0:T(8,128)S(1)}, f32[544,128]{1,0:T(8,128)S(1)}, u32[]{:S(2)}, u32[]{:S(2)}) collective-permute-start(f32[544,128]{1,0:T(8,128)S(1)} %get-tuple-element.8), channel_id=1, source_target_pairs={{0,1},{1,0},{2,3},{3,2},{4,5},{5,4},{6,7},{7,6},{8,9},{9,8},{10,11... | collective-permute-start | bytes 835592 | tf_op jit(solution)/shard_map/ppermute | solution.py:111
  117.5 1.2 collective-permute-done
  118.7 20.2 %all_to_all.21 = f32[32,1,2176]{2,1,0:T(1,128)S(1)} all-to-all(f32[32,1,2176]{2,1,0:T(1,128)S(1)} %bitcast.8), channel_id=1, replica_groups=mesh['x'=4,'y'=8,'z'=8,'core'=2] {'x','z'}, dimensions={0} | all-to-all | bytes 557056 | tf_op jit(solution)/shard_map/all_to_all | solution.py:107
  138.9 0.2 reduce_sum.18
  139.2 11.2 %all_to_all.22 = f32[8,1,2176]{2,1,0:T(1,128)S(1)} all-to-all(f32[8,1,2176]{2,1,0:T(1,128)S(1)} %broadcast_in_dim.4), channel_id=1, replica_groups=mesh['x'=4,'y'=8,'z'=8,'core'=2] {'y'}, dimensions={0} | all-to-all | bytes 139264 | tf_op jit(solution)/shard_map/all_to_all | solution.py:107
  150.4 0.1 reduce_sum.19
  150.4 0.1 broadcast_in_dim.5
  150.6 16.7 %all_to_all.23 = f32[32,1,2176]{2,1,0:T(1,128)S(1)} all-to-all(f32[32,1,2176]{2,1,0:T(1,128)S(1)} %broadcast_in_dim.5), channel_id=1, replica_groups=mesh['x'=4,'y'=8,'z'=8,'core'=2] {'x','z'}, dimensions={0} | all-to-all | bytes 557056 | tf_op jit(solution)/shard_map/all_to_all | solution.py:107
  167.3 6.9 %collective-permute-start.1 = (f32[544,128]{1,0:T(8,128)S(1)}, f32[544,128]{1,0:T(8,128)S(1)}, u32[]{:S(2)}, u32[]{:S(2)}) collective-permute-start(f32[544,128]{1,0:T(8,128)S(1)} %bitcast.4), channel_id=1, source_target_pairs={{0,1},{1,0},{2,3},{3,2},{4,5},{5,4},{6,7},{7,6},{8,9},{9,8},{10,11... | collective-permute-start | bytes 835592 | tf_op jit(solution)/shard_map/ppermute | solution.py:111
  174.2 1.2 collective-permute-done.1.other_ref
  175.3 0.0 copy-done.2
  175.3 0.0 copy-start.1
  175.3 2.2 %copy-done.1 = bf16[32,2,16,2048]{3,2,1,0:T(8,128)(2,1)S(1)} copy-done((bf16[32,2,16,2048]{3,2,1,0:T(8,128)(2,1)S(1)}, bf16[32,2,16,2048]{3,2,1,0:T(8,128)(2,1)}, u32[]{:S(2)}) %copy-start.1) | copy-done | bytes 4194328
  177.5 14.2 %subspace_and_core.1 = bf16[128,4096]{1,0:T(8,128)(2,1)S(1)} custom-call(f32[544,128]{1,0:T(8,128)S(1)} %bitcast.5, f32[544,128]{1,0:T(8,128)S(1)} %collective-permute-done.1.other_ref, f32[512,128]{1,0:T(8,128)S(1)} %copy-done.2, bf16[32,2,16,2048]{3,2,1,0:T(8,128)(2,1)S(1)} %copy-done.1), custom_call_target="tpu_custom_call" | custom-call | tf_op jit(solution)/shard_map/subspace_and_core/pallas_call | solution.py:200
  191.7 1.6 reshape.25
  (2 shorter events, 0.1 us)
Async XLA Ops:
  106.8 68.5 %copy-start.2 = (f32[512,128]{1,0:T(8,128)S(1)}, f32[512,128]{1,0:T(8,128)}, u32[]{:S(2)}) copy-start(f32[512,128]{1,0:T(8,128)} %start_ref.1) | copy-start | bytes 786436
  108.7 1.9 %copy-start = (bf16[32,2,16,2048]{3,2,1,0:T(8,128)(2,1)}, bf16[32,2,16,2048]{3,2,1,0:T(8,128)(2,1)S(1)}, u32[]{:S(2)}) copy-start(bf16[32,2,16,2048]{3,2,1,0:T(8,128)(2,1)S(1)} %all_to_all.20.u_ref) | copy-start | bytes 12582916
  110.7 8.0 %collective-permute-start = (f32[544,128]{1,0:T(8,128)S(1)}, f32[544,128]{1,0:T(8,128)S(1)}, u32[]{:S(2)}, u32[]{:S(2)}) collective-permute-start(f32[544,128]{1,0:T(8,128)S(1)} %get-tuple-element.8), channel_id=1, source_target_pairs={{0,1},{1,0},{2,3},{3,2},{4,5},{5,4},{6,7},{7,6},{8,9},{9,8},{10,11... | collective-permute-start | bytes 835592 | tf_op jit(solution)/shard_map/ppermute | solution.py:111
  167.3 8.0 %collective-permute-start.1 = (f32[544,128]{1,0:T(8,128)S(1)}, f32[544,128]{1,0:T(8,128)S(1)}, u32[]{:S(2)}, u32[]{:S(2)}) collective-permute-start(f32[544,128]{1,0:T(8,128)S(1)} %bitcast.4), channel_id=1, source_target_pairs={{0,1},{1,0},{2,3},{3,2},{4,5},{5,4},{6,7},{7,6},{8,9},{9,8},{10,11... | collective-permute-start | bytes 835592 | tf_op jit(solution)/shard_map/ppermute | solution.py:111
  175.3 2.2 %copy-start.1 = (bf16[32,2,16,2048]{3,2,1,0:T(8,128)(2,1)S(1)}, bf16[32,2,16,2048]{3,2,1,0:T(8,128)(2,1)}, u32[]{:S(2)}) copy-start(bf16[32,2,16,2048]{3,2,1,0:T(8,128)(2,1)} %copy-done) | copy-start | bytes 12582916

commit v3 on v2

--- a/solution.py
+++ b/solution.py
@@ -8,12 +8,14 @@
 ITERS = 2
 SUB = 8
 TILE = 128
+TH_STEP = 16
+CELLS = 1024
 AXES = ("x", "y", "z", "core")
 SIZES = (4, 8, 8, 2)
 RAD = ("x", "y")
 WIDE = ("x", "z")
 MID = ("y",)
-VMEM_LIMIT = 24 * 2**20
+VMEM_LIMIT = 52 * 2**20
 
 
 def group(names):
@@ -31,22 +33,71 @@
     return (lax.broadcasted_iota(jnp.int32, (TILE, TILE), d) for d in (0, 1))
 
 
-def gram_kernel(u_ref, keep_ref, send_ref, acc_ref):
+def regroup_kernel(field_ref, out_ref, held_ref, moved_ref, sems, out_sems):
+    radii, th, _ = field_ref.shape
+    rows = radii * TH_STEP
+    copies = []
+    for n in range(th // TH_STEP):
+        part = field_ref.at[:, pl.ds(TH_STEP * n, TH_STEP)]
+        copies.append(pltpu.make_async_copy(part, held_ref.at[n], sems.at[n]))
+        copies[-1].start()
+    to = lax.broadcasted_iota(jnp.int32, (rows, rows), 0)
+    source = lax.broadcasted_iota(jnp.int32, (rows, rows), 1)
+    moved = jnp.where((to // radii == source % TH_STEP) & (to % radii == source // TH_STEP), 1.0, 0.0)
+    moved = moved.astype(jnp.bfloat16)
+    results = []
+    for n, copy in enumerate(copies):
+        copy.wait()
+        x = held_ref[n].reshape(rows, held_ref.shape[-1])
+        y = jnp.dot(moved, x, preferred_element_type=jnp.float32).astype(jnp.bfloat16)
+        moved_ref[n] = y.reshape(TH_STEP, radii, held_ref.shape[-1])
+        part = out_ref.at[pl.ds(TH_STEP * n, TH_STEP)]
+        results.append(pltpu.make_async_copy(moved_ref.at[n], part, out_sems.at[n]))
+        results[-1].start()
+    for result in results:
+        result.wait()
+
+
+def by_colatitude(field):
+    radii, th, ph = field.shape
+    parts = th // TH_STEP
+    return pl.pallas_call(
+        regroup_kernel,
+        in_specs=[pl.BlockSpec(memory_space=pltpu.HBM)],
+        out_specs=pl.BlockSpec(memory_space=pltpu.HBM),
+        out_shape=jax.ShapeDtypeStruct((th, radii, ph), field.dtype),
+        scratch_shapes=[
+            pltpu.VMEM((parts, radii, TH_STEP, ph), field.dtype),
+            pltpu.VMEM((parts, TH_STEP, radii, ph), field.dtype),
+            pltpu.SemaphoreType.DMA((parts,)),
+            pltpu.SemaphoreType.DMA((parts,)),
+        ],
+        compiler_params=pltpu.CompilerParams(vmem_limit_bytes=VMEM_LIMIT),
+        name="by_colatitude",
+    )(field)
+
+
+def gram_kernel(u_ref, keep_ref, send_ref, acc_ref, held_ref, sems):
     src, th, radii, ph = u_ref.shape
     order = src * radii
     half = order // 2
-    cells = 1024
-    for t in range(th):
-        for c in range(ph // cells):
-            u = u_ref[:, t, :, cells * c:cells * (c + 1)].reshape(order, cells)
-            top = lax.dot_general(u[:half], u, (((1,), (1,)), ((), ())), preferred_element_type=jnp.float32)
-            low = lax.dot_general(u[half:], u[half:], (((1,), (1,)), ((), ())), preferred_element_type=jnp.float32)
-            if t == 0 and c == 0:
-                acc_ref[:half] = top
-                acc_ref[half:, half:] = low
-            else:
-                acc_ref[:half] += top
-                acc_ref[half:, half:] += low
+    copies = []
+    for n in range(th * (ph // CELLS)):
+        t, c = divmod(n, ph // CELLS)
+        part = u_ref.at[:, t, :, pl.ds(CELLS * c, CELLS)]
+        copies.append(pltpu.make_async_copy(part, held_ref.at[n], sems.at[n]))
+        copies[-1].start()
+    for n, copy in enumerate(copies):
+        copy.wait()
+        u = held_ref[n].reshape(order, CELLS)
+        top = lax.dot_general(u[:half], u, (((1,), (1,)), ((), ())), preferred_element_type=jnp.float32)
+        low = lax.dot_general(u[half:], u[half:], (((1,), (1,)), ((), ())), preferred_element_type=jnp.float32)
+        if n == 0:
+            acc_ref[:half] = top
+            acc_ref[half:, half:] = low
+        else:
+            acc_ref[:half] += top
+            acc_ref[half:, half:] += low
     row, col = tile_iota()
 
     def block(i, j):
@@ -72,14 +123,19 @@
 def partial_gram(regrouped):
     src, th, radii, ph = regrouped.shape
     order = src * radii
+    parts = th * (ph // CELLS)
     vmem = pl.BlockSpec(memory_space=pltpu.VMEM)
     out = jax.ShapeDtypeStruct((4 * TILE + group(WIDE), TILE), jnp.float32)
     return pl.pallas_call(
         gram_kernel,
-        in_specs=[vmem],
+        in_specs=[pl.BlockSpec(memory_space=pltpu.HBM)],
         out_specs=[vmem, vmem],
         out_shape=[out, out],
-        scratch_shapes=[pltpu.VMEM((order, order), jnp.float32)],
+        scratch_shapes=[
+            pltpu.VMEM((order, order), jnp.float32),
+            pltpu.VMEM((parts, src, radii, CELLS), jnp.bfloat16),
+            pltpu.SemaphoreType.DMA((parts,)),
+        ],
         compiler_params=pltpu.CompilerParams(vmem_limit_bytes=VMEM_LIMIT),
         name="gram",
     )(regrouped)
@@ -167,7 +223,9 @@
     )
 
 
-def core_kernel(mine_ref, other_ref, start_ref, u_ref, out_ref, gram_ref, basis_ref):
+def core_kernel(mine_ref, other_ref, start_ref, u_ref, out_ref, gram_ref, basis_ref, held_ref, sem):
+    copy = pltpu.make_async_copy(u_ref, held_ref, sem)
+    copy.start()
     core = lax.axis_index("core")
     for own in (0, 1):
         @pl.when(core == own)
@@ -184,11 +242,12 @@
 
     lax.fori_loop(0, ITERS, step, 0)
     narrow = basis_ref[...].T.astype(jnp.bfloat16)
-    src, th, radii, ph = u_ref.shape
+    copy.wait()
+    src, th, radii, ph = held_ref.shape
     cells = 512
     for t in range(th):
         for c in range(ph // cells):
-            u = u_ref[:, t, :, cells * c:cells * (c + 1)].reshape(src * radii, cells)
+            u = held_ref[:, t, :, cells * c:cells * (c + 1)].reshape(src * radii, cells)
             core = jnp.dot(narrow, u, preferred_element_type=jnp.float32)
             out_ref[:, t * ph + cells * c:t * ph + cells * (c + 1)] = core.astype(jnp.bfloat16)
 
@@ -199,10 +258,15 @@
     vmem = pl.BlockSpec(memory_space=pltpu.VMEM)
     return pl.pallas_call(
         core_kernel,
-        in_specs=[vmem] * 4,
+        in_specs=[vmem] * 3 + [pl.BlockSpec(memory_space=pltpu.HBM)],
         out_specs=vmem,
         out_shape=jax.ShapeDtypeStruct((rank, th * ph), jnp.bfloat16),
-        scratch_shapes=[pltpu.VMEM((order, order), jnp.float32), pltpu.VMEM((order, rank), jnp.float32)],
+        scratch_shapes=[
+            pltpu.VMEM((order, order), jnp.float32),
+            pltpu.VMEM((order, rank), jnp.float32),
+            pltpu.VMEM(regrouped.shape, jnp.bfloat16),
+            pltpu.SemaphoreType.DMA,
+        ],
         compiler_params=pltpu.CompilerParams(vmem_limit_bytes=VMEM_LIMIT),
         name="subspace_and_core",
     )(mine, other, start, regrouped)
@@ -211,7 +275,7 @@
 def on_device(field, start):
     radii, th, ph = field.shape
     owners = group(RAD)
-    sent = field.transpose(1, 0, 2).reshape(owners, th // owners, radii, ph)
+    sent = by_colatitude(field).reshape(owners, th // owners, radii, ph)
     regrouped = swap(sent, RAD)
     mine, other = sum_everywhere(*partial_gram(regrouped))
     core = core_of(mine, other, start, regrouped)

time: 194 us -> 192 us (0.990)
  local copies, waits for them, and re-layouts: 10.4 us -> 1.77 us
  Pallas kernels: 16 us -> 22.6 us
    pallas_call x2 -> x3, Pallas kernels: 16 us -> 22.6 us  [the longest x1 14.2 us: core_of(): pl.pallas_call(core_kernel, in_specs=[vmem] * 3 + [pl.BlockSpec(memory_sp...]
    transpose x1 -> x0, local copies, waits for them, and re-layouts: 4.49 us -> none  [on_device(): sent = field.transpose(1, 0, 2).reshape(owners, th // owners, radii, ph)]
    unnamed x6 -> x2, local copies, waits for them, and re-layouts: 4.13 us -> 0.01 us
where the time goes in v3:
time: 192 us
  blocking collectives  151 us (79%)
  Pallas kernels  22.6 us (12%)
  starting transfers between devices  13.8 us (7%)
  waiting for transfers between devices  2.33 us (1%)
    all_to_all x4, blocking collectives, swap(): return lax.all_to_all(x, names, split_axis=0, concat_axis=0, tiled=True)  151 us
    pallas_call x1, Pallas kernels, core_of(): pl.pallas_call(core_kernel, in_specs=[vmem] * 3 + [pl.BlockSpec(memory_sp...  14.2 us
    ppermute x2, starting transfers between devices, swap_core(): return lax.ppermute(x, 'core', [(0, 1), (1, 0)])  13.8 us
    pallas_call x1, Pallas kernels, partial_gram(): pl.pallas_call(gram_kernel, in_specs=[pl.BlockSpec(memory_space=pltpu.HBM...  4.33 us
    pallas_call x1, Pallas kernels, by_colatitude(): pl.pallas_call(regroup_kernel, in_specs=[pl.BlockSpec(memory_space=pltpu....  4.05 us
  transfers between devices with their start and end apart: 2, of which 2 were waited for; matrix products, arithmetic and copies ran while one was open for 0% of the time, Pallas kernels for 0%

profile of v3, /device:TPU:1, one launch (start us, length us, event | category | flops | bytes accessed | tf_op | source)
XLA Modules:
  0.0 191.5 jit_solution(17351943534841122872)
XLA Ops:
  0.0 4.1 %by_colatitude.1 = bf16[64,16,2048]{2,1,0:T(8,128)(2,1)} custom-call(bf16[16,64,2048]{2,1,0:T(8,128)(2,1)} %field_ref.1), custom_call_target="tpu_custom_call" | custom-call | tf_op jit(solution)/shard_map/by_colatitude/pallas_call | solution.py:64
  4.1 102.7 %all_to_all.20.u_ref = bf16[32,2,16,2048]{3,2,1,0:T(8,128)(2,1)} all-to-all(bf16[32,2,16,2048]{3,2,1,0:T(8,128)(2,1)} %bitcast.5), channel_id=1, replica_groups=mesh['x'=4,'y'=8,'z'=8,'core'=2] {'x','y'}, dimensions={0} | all-to-all | bytes 8388608 | tf_op jit(solution)/shard_map/all_to_all | solution.py:163
  106.7 0.0 copy-start
  106.7 4.3 %gram.1 = (f32[544,128]{1,0:T(8,128)S(1)}, f32[544,128]{1,0:T(8,128)S(1)}) custom-call(bf16[32,2,16,2048]{3,2,1,0:T(8,128)(2,1)} %all_to_all.20.u_ref), custom_call_target="tpu_custom_call" | custom-call | tf_op jit(solution)/shard_map/gram/pallas_call | solution.py:129
  111.1 6.9 %collective-permute-start = (f32[544,128]{1,0:T(8,128)S(1)}, f32[544,128]{1,0:T(8,128)S(1)}, u32[]{:S(2)}, u32[]{:S(2)}) collective-permute-start(f32[544,128]{1,0:T(8,128)S(1)} %get-tuple-element.8), channel_id=1, source_target_pairs={{0,1},{1,0},{2,3},{3,2},{4,5},{5,4},{6,7},{7,6},{8,9},{9,8},{10,11... | collective-permute-start | bytes 835592 | tf_op jit(solution)/shard_map/ppermute | solution.py:167
  118.0 1.2 collective-permute-done
  119.2 20.1 %all_to_all.21 = f32[32,1,2176]{2,1,0:T(1,128)S(1)} all-to-all(f32[32,1,2176]{2,1,0:T(1,128)S(1)} %bitcast.6), channel_id=1, replica_groups=mesh['x'=4,'y'=8,'z'=8,'core'=2] {'x','z'}, dimensions={0} | all-to-all | bytes 557056 | tf_op jit(solution)/shard_map/all_to_all | solution.py:163
  139.3 0.2 reduce_sum.18
  139.5 11.2 %all_to_all.22 = f32[8,1,2176]{2,1,0:T(1,128)S(1)} all-to-all(f32[8,1,2176]{2,1,0:T(1,128)S(1)} %broadcast_in_dim.4), channel_id=1, replica_groups=mesh['x'=4,'y'=8,'z'=8,'core'=2] {'y'}, dimensions={0} | all-to-all | bytes 139264 | tf_op jit(solution)/shard_map/all_to_all | solution.py:163
  150.8 0.1 reduce_sum.19
  150.8 0.1 broadcast_in_dim.5
  151.0 16.7 %all_to_all.23 = f32[32,1,2176]{2,1,0:T(1,128)S(1)} all-to-all(f32[32,1,2176]{2,1,0:T(1,128)S(1)} %broadcast_in_dim.5), channel_id=1, replica_groups=mesh['x'=4,'y'=8,'z'=8,'core'=2] {'x','z'}, dimensions={0} | all-to-all | bytes 557056 | tf_op jit(solution)/shard_map/all_to_all | solution.py:163
  167.7 6.9 %collective-permute-start.1 = (f32[544,128]{1,0:T(8,128)S(1)}, f32[544,128]{1,0:T(8,128)S(1)}, u32[]{:S(2)}, u32[]{:S(2)}) collective-permute-start(f32[544,128]{1,0:T(8,128)S(1)} %bitcast.3), channel_id=1, source_target_pairs={{0,1},{1,0},{2,3},{3,2},{4,5},{5,4},{6,7},{7,6},{8,9},{9,8},{10,11... | collective-permute-start | bytes 835592 | tf_op jit(solution)/shard_map/ppermute | solution.py:167
  174.6 1.2 collective-permute-done.1.other_ref
  175.7 0.0 copy-done
  175.7 14.2 %subspace_and_core.1 = bf16[128,4096]{1,0:T(8,128)(2,1)S(1)} custom-call(f32[544,128]{1,0:T(8,128)S(1)} %bitcast.4, f32[544,128]{1,0:T(8,128)S(1)} %collective-permute-done.1.other_ref, f32[512,128]{1,0:T(8,128)S(1)} %copy-done, bf16[32,2,16,2048]{3,2,1,0:T(8,128)(2,1)} %all_to_all.20.u_ref), custom_call_target="tpu_custom_call" | custom-call | tf_op jit(solution)/shard_map/subspace_and_core/pallas_call | solution.py:259
  190.0 1.6 reshape.25
  (2 shorter events, 0.1 us)
Async XLA Ops:
  106.7 69.0 %copy-start = (f32[512,128]{1,0:T(8,128)S(1)}, f32[512,128]{1,0:T(8,128)}, u32[]{:S(2)}) copy-start(f32[512,128]{1,0:T(8,128)} %start_ref.1) | copy-start | bytes 786436
  111.1 8.1 %collective-permute-start = (f32[544,128]{1,0:T(8,128)S(1)}, f32[544,128]{1,0:T(8,128)S(1)}, u32[]{:S(2)}, u32[]{:S(2)}) collective-permute-start(f32[544,128]{1,0:T(8,128)S(1)} %get-tuple-element.8), channel_id=1, source_target_pairs={{0,1},{1,0},{2,3},{3,2},{4,5},{5,4},{6,7},{7,6},{8,9},{9,8},{10,11... | collective-permute-start | bytes 835592 | tf_op jit(solution)/shard_map/ppermute | solution.py:167
  167.7 8.0 %collective-permute-start.1 = (f32[544,128]{1,0:T(8,128)S(1)}, f32[544,128]{1,0:T(8,128)S(1)}, u32[]{:S(2)}, u32[]{:S(2)}) collective-permute-start(f32[544,128]{1,0:T(8,128)S(1)} %bitcast.3), channel_id=1, source_target_pairs={{0,1},{1,0},{2,3},{3,2},{4,5},{5,4},{6,7},{7,6},{8,9},{9,8},{10,11... | collective-permute-start | bytes 835592 | tf_op jit(solution)/shard_map/ppermute | solution.py:167

commit v4 on v3

--- a/solution.py
+++ b/solution.py
@@ -7,15 +7,19 @@
 
 ITERS = 2
 SUB = 8
+BLOCK = 16
 TILE = 128
 TH_STEP = 16
 CELLS = 1024
+AHEAD = 4
 AXES = ("x", "y", "z", "core")
 SIZES = (4, 8, 8, 2)
 RAD = ("x", "y")
 WIDE = ("x", "z")
 MID = ("y",)
 VMEM_LIMIT = 52 * 2**20
+GRAM_LIMIT = 46 * 2**20
+HELD_ROOM = 2
 
 
 def group(names):
@@ -40,7 +44,8 @@
     for n in range(th // TH_STEP):
         part = field_ref.at[:, pl.ds(TH_STEP * n, TH_STEP)]
         copies.append(pltpu.make_async_copy(part, held_ref.at[n], sems.at[n]))
-        copies[-1].start()
+    for copy in copies[:AHEAD]:
+        copy.start()
     to = lax.broadcasted_iota(jnp.int32, (rows, rows), 0)
     source = lax.broadcasted_iota(jnp.int32, (rows, rows), 1)
     moved = jnp.where((to // radii == source % TH_STEP) & (to % radii == source // TH_STEP), 1.0, 0.0)
@@ -48,6 +53,8 @@
     results = []
     for n, copy in enumerate(copies):
         copy.wait()
+        for later in copies[n + AHEAD:n + AHEAD + 1]:
+            later.start()
         x = held_ref[n].reshape(rows, held_ref.shape[-1])
         y = jnp.dot(moved, x, preferred_element_type=jnp.float32).astype(jnp.bfloat16)
         moved_ref[n] = y.reshape(TH_STEP, radii, held_ref.shape[-1])
@@ -77,19 +84,15 @@
     )(field)
 
 
-def gram_kernel(u_ref, keep_ref, send_ref, acc_ref, held_ref, sems):
+def gram_kernel(u_ref, keep_ref, send_ref, held_ref, acc_ref, sem):
     src, th, radii, ph = u_ref.shape
+    copy = pltpu.make_async_copy(u_ref, held_ref.at[pl.ds(0, src)], sem)
+    copy.start()
     order = src * radii
     half = order // 2
-    copies = []
     for n in range(th * (ph // CELLS)):
         t, c = divmod(n, ph // CELLS)
-        part = u_ref.at[:, t, :, pl.ds(CELLS * c, CELLS)]
-        copies.append(pltpu.make_async_copy(part, held_ref.at[n], sems.at[n]))
-        copies[-1].start()
-    for n, copy in enumerate(copies):
-        copy.wait()
-        u = held_ref[n].reshape(order, CELLS)
+        u = u_ref[:, t, :, CELLS * c:CELLS * (c + 1)].reshape(order, CELLS)
         top = lax.dot_general(u[:half], u, (((1,), (1,)), ((), ())), preferred_element_type=jnp.float32)
         low = lax.dot_general(u[half:], u[half:], (((1,), (1,)), ((), ())), preferred_element_type=jnp.float32)
         if n == 0:
@@ -119,24 +122,21 @@
             pack(keep_ref, halves()[own])
             pack(send_ref, halves()[1 - own])
 
+    copy.wait()
+
 
 def partial_gram(regrouped):
     src, th, radii, ph = regrouped.shape
     order = src * radii
-    parts = th * (ph // CELLS)
     vmem = pl.BlockSpec(memory_space=pltpu.VMEM)
     out = jax.ShapeDtypeStruct((4 * TILE + group(WIDE), TILE), jnp.float32)
     return pl.pallas_call(
         gram_kernel,
-        in_specs=[pl.BlockSpec(memory_space=pltpu.HBM)],
-        out_specs=[vmem, vmem],
-        out_shape=[out, out],
-        scratch_shapes=[
-            pltpu.VMEM((order, order), jnp.float32),
-            pltpu.VMEM((parts, src, radii, CELLS), jnp.bfloat16),
-            pltpu.SemaphoreType.DMA((parts,)),
-        ],
-        compiler_params=pltpu.CompilerParams(vmem_limit_bytes=VMEM_LIMIT),
+        in_specs=[vmem],
+        out_specs=[vmem, vmem, pl.BlockSpec(memory_space=pltpu.HBM)],
+        out_shape=[out, out, jax.ShapeDtypeStruct((HELD_ROOM * src, th, radii, ph), regrouped.dtype)],
+        scratch_shapes=[pltpu.VMEM((order, order), jnp.float32), pltpu.SemaphoreType.DMA],
+        compiler_params=pltpu.CompilerParams(vmem_limit_bytes=GRAM_LIMIT),
         name="gram",
     )(regrouped)
 
@@ -179,13 +179,27 @@
     return mine, swap_core(mine)
 
 
+def split(x):
+    one = x.astype(jnp.bfloat16)
+    rest = x - one.astype(jnp.float32)
+    two = rest.astype(jnp.bfloat16)
+    return one, two, (rest - two.astype(jnp.float32)).astype(jnp.bfloat16)
+
+
+def outer(a, b):
+    a1, a2, a3 = split(a)
+    b1, b2, b3 = split(b)
+    return lax.dot_general(
+        jnp.concatenate([a1, a1, a2, a2, a1, a3], axis=0),
+        jnp.concatenate([b1, b2, b1, b2, b3, b1], axis=0),
+        (((0,), (0,)), ((), ())), preferred_element_type=jnp.float32,
+    )
+
+
 def inverse_lower(inner):
     n = inner.shape[0]
-    parts = n // SUB
     row = lax.broadcasted_iota(jnp.int32, (SUB, n), 0)
     col = lax.broadcasted_iota(jnp.int32, (SUB, n), 1)
-    left = [inner[SUB * q:SUB * (q + 1)] for q in range(parts)]
-    right = [jnp.where(col == row + SUB * q, 1.0, 0.0) for q in range(parts)]
 
     def spread(x, c):
         return jnp.broadcast_to(x[:, c:c + 1], (SUB, n))
@@ -193,27 +207,58 @@
     def pick(x, r):
         return jnp.broadcast_to(x[r:r + 1], (SUB, n))
 
-    for p in range(parts):
-        columns = {q: [spread(left[q], SUB * p + j) for j in range(SUB)] for q in range(p, parts)}
-        pivots = jnp.ones((SUB, n), jnp.float32)
-        for j in range(SUB):
-            own = columns[p]
-            pivot = pick(own[j], j)
-            inv = 1.0 / pivot
-            pivots = jnp.where(row == j, pivot, pivots)
-            lead_left = pick(left[p], j)
-            lead_right = pick(right[p], j)
-            lead = [pick(own[c], j) for c in range(j + 1, SUB)]
-            for q in range(p, parts):
-                times = columns[q][j] * inv
-                if q == p:
-                    times = jnp.where(row > j, times, 0.0)
-                left[q] = left[q] - times * lead_left
-                right[q] = right[q] - times * lead_right
+    def panels(x, count):
+        return [x[SUB * q:SUB * (q + 1)] for q in range(count)]
+
+    done = []
+    left_rest, right_rest = inner, jnp.zeros_like(inner)
+    for start in range(0, n, BLOCK):
+        count = BLOCK // SUB
+        left = panels(left_rest, count)
+        right = [x + jnp.where(col == row + start + SUB * q, 1.0, 0.0) for q, x in enumerate(panels(right_rest, count))]
+        own = [spread(left[0], start + j) for j in range(SUB)]
+        scales, roots = [], []
+        for p in range(count):
+            at = start + SUB * p
+            more = p + 1 < count
+            if more:
+                below = [spread(left[p + 1], at + j) for j in range(SUB)]
+                after = [spread(left[p + 1], at + SUB + j) for j in range(SUB)]
+            scale = jnp.ones((SUB, n), jnp.float32)
+            pivots = jnp.ones((SUB, n), jnp.float32)
+            for j in range(SUB):
+                pivot = pick(own[j], j)
+                inv = 1.0 / pivot
+                pivots = jnp.where(row == j, pivot, pivots)
+                scale = jnp.where(row == j, inv, scale)
+                lead_left, lead_right = pick(left[p], j), pick(right[p], j)
+                lead = {c: pick(own[c], j) for c in range(j + 1, SUB)}
+                times = jnp.where(row > j, own[j], 0.0) * inv
                 for c in range(j + 1, SUB):
-                    columns[q][c] = columns[q][c] - times * lead[c - j - 1]
-        right[p] = right[p] / jnp.sqrt(pivots)
-    return jnp.concatenate(right, axis=0)
+                    own[c] = own[c] - times * lead[c]
+                left[p] = left[p] - times * lead_left
+                right[p] = right[p] - times * lead_right
+                if more:
+                    times = below[j] * inv
+                    for c in range(SUB):
+                        after[c] = after[c] - times * pick(below[j], c)
+                    for c in range(j + 1, SUB):
+                        below[c] = below[c] - times * lead[c]
+                    left[p + 1] = left[p + 1] - times * lead_left
+                    right[p + 1] = right[p + 1] - times * lead_right
+            scales.append(scale)
+            roots.append(jnp.sqrt(pivots))
+            if more:
+                own = after
+        left_block = jnp.concatenate(left, axis=0)
+        right_block = jnp.concatenate(right, axis=0)
+        done.append(right_block / jnp.concatenate(roots, axis=0))
+        if start + BLOCK < n:
+            scaled = left_block * jnp.concatenate(scales, axis=0)
+            change = outer(scaled, jnp.concatenate([left_block, right_block], axis=1))[start + BLOCK:]
+            left_rest = left_rest[BLOCK:] - change[:, :n]
+            right_rest = right_rest[BLOCK:] - change[:, n:]
+    return jnp.concatenate(done, axis=0)
 
 
 def exact(a, b, dims):
@@ -224,7 +269,7 @@
 
 
 def core_kernel(mine_ref, other_ref, start_ref, u_ref, out_ref, gram_ref, basis_ref, held_ref, sem):
-    copy = pltpu.make_async_copy(u_ref, held_ref, sem)
+    copy = pltpu.make_async_copy(u_ref.at[pl.ds(0, held_ref.shape[0])], held_ref, sem)
     copy.start()
     core = lax.axis_index("core")
     for own in (0, 1):
@@ -232,16 +277,16 @@
         def _():
             unpack_half(mine_ref[...], halves()[own], gram_ref)
             unpack_half(other_ref[...], halves()[1 - own], gram_ref)
-    basis_ref[...] = start_ref[...]
+    basis_ref[...] = start_ref[...].T
 
     def step(_, carry):
-        grown = exact(gram_ref[...], basis_ref[...], (1, 0))
-        inner = exact(grown, grown, (0, 0))
-        basis_ref[...] = exact(grown, inverse_lower(inner), (1, 1))
+        grown = exact(basis_ref[...], gram_ref[...], (1, 0))
+        inner = exact(grown, grown, (1, 1))
+        basis_ref[...] = exact(inverse_lower(inner), grown, (1, 0))
         return carry
 
     lax.fori_loop(0, ITERS, step, 0)
-    narrow = basis_ref[...].T.astype(jnp.bfloat16)
+    narrow = basis_ref[...].astype(jnp.bfloat16)
     copy.wait()
     src, th, radii, ph = held_ref.shape
     cells = 512
@@ -252,9 +297,10 @@
             out_ref[:, t * ph + cells * c:t * ph + cells * (c + 1)] = core.astype(jnp.bfloat16)
 
 
-def core_of(mine, other, start, regrouped):
+def core_of(mine, other, start, held):
     order, rank = start.shape
-    src, th, radii, ph = regrouped.shape
+    src, th, radii, ph = held.shape
+    src //= HELD_ROOM
     vmem = pl.BlockSpec(memory_space=pltpu.VMEM)
     return pl.pallas_call(
         core_kernel,
@@ -263,13 +309,13 @@
         out_shape=jax.ShapeDtypeStruct((rank, th * ph), jnp.bfloat16),
         scratch_shapes=[
             pltpu.VMEM((order, order), jnp.float32),
-            pltpu.VMEM((order, rank), jnp.float32),
-            pltpu.VMEM(regrouped.shape, jnp.bfloat16),
+            pltpu.VMEM((rank, order), jnp.float32),
+            pltpu.VMEM((src, th, radii, ph), jnp.bfloat16),
             pltpu.SemaphoreType.DMA,
         ],
         compiler_params=pltpu.CompilerParams(vmem_limit_bytes=VMEM_LIMIT),
         name="subspace_and_core",
-    )(mine, other, start, regrouped)
+    )(mine, other, start, held)
 
 
 def on_device(field, start):
@@ -277,8 +323,9 @@
     owners = group(RAD)
     sent = by_colatitude(field).reshape(owners, th // owners, radii, ph)
     regrouped = swap(sent, RAD)
-    mine, other = sum_everywhere(*partial_gram(regrouped))
-    core = core_of(mine, other, start, regrouped)
+    keep, send, held = partial_gram(regrouped)
+    mine, other = sum_everywhere(keep, send)
+    core = core_of(mine, other, start, held)
     return core.reshape(start.shape[1], th // owners, ph)
 
 

time: 192 us -> 186 us (0.969)
  Pallas kernels: 22.6 us -> 16.7 us
    pallas_call x1, Pallas kernels: 14.2 us -> 10.8 us  [core_of(): pl.pallas_call(core_kernel, in_specs=[vmem] * 3 + [pl.BlockSpec(memory_sp...]
    pallas_call x1, Pallas kernels: 4.33 us -> 1.93 us  [partial_gram(): pl.pallas_call(gram_kernel, in_specs=[vmem], out_specs=[vmem, vmem, pl.Bl...]
where the time goes in v4:
time: 186 us
  blocking collectives  151 us (81%)
  Pallas kernels  16.7 us (9%)
  starting transfers between devices  13.7 us (7%)
  waiting for transfers between devices  2.33 us (1%)
    all_to_all x4, blocking collectives, swap(): return lax.all_to_all(x, names, split_axis=0, concat_axis=0, tiled=True)  151 us
    ppermute x2, starting transfers between devices, swap_core(): return lax.ppermute(x, 'core', [(0, 1), (1, 0)])  13.7 us
    pallas_call x1, Pallas kernels, core_of(): pl.pallas_call(core_kernel, in_specs=[vmem] * 3 + [pl.BlockSpec(memory_sp...  10.8 us
    pallas_call x1, Pallas kernels, by_colatitude(): pl.pallas_call(regroup_kernel, in_specs=[pl.BlockSpec(memory_space=pltpu....  4.05 us
  transfers between devices with their start and end apart: 2, of which 2 were waited for; matrix products, arithmetic and copies ran while one was open for 0% of the time, Pallas kernels for 0%

profile of v4, /device:TPU:1, one launch (start us, length us, event | category | flops | bytes accessed | tf_op | source)
XLA Modules:
  0.0 185.6 jit_solution(11647461853980778092)
XLA Ops:
  0.0 4.1 %by_colatitude.1 = bf16[64,16,2048]{2,1,0:T(8,128)(2,1)} custom-call(bf16[16,64,2048]{2,1,0:T(8,128)(2,1)} %field_ref.1), custom_call_target="tpu_custom_call" | custom-call | tf_op jit(solution)/shard_map/by_colatitude/pallas_call | solution.py:71
  4.1 102.6 %all_to_all.20.u_ref = bf16[32,2,16,2048]{3,2,1,0:T(8,128)(2,1)S(1)} all-to-all(bf16[32,2,16,2048]{3,2,1,0:T(8,128)(2,1)} %bitcast.5), channel_id=1, replica_groups=mesh['x'=4,'y'=8,'z'=8,'core'=2] {'x','y'}, dimensions={0} | all-to-all | bytes 8388608 | tf_op jit(solution)/shard_map/all_to_all | solution.py:163
  106.6 0.0 copy-start
  106.6 1.9 %gram.1 = (f32[544,128]{1,0:T(8,128)S(1)}, f32[544,128]{1,0:T(8,128)S(1)}, bf16[64,2,16,2048]{3,2,1,0:T(8,128)(2,1)}) custom-call(bf16[32,2,16,2048]{3,2,1,0:T(8,128)(2,1)S(1)} %all_to_all.20.u_ref), custom_call_target="tpu_custom_call" | custom-call | tf_op jit(solution)/shard_map/gram/pallas_call | solution.py:133
  108.6 6.9 %collective-permute-start = (f32[544,128]{1,0:T(8,128)S(1)}, f32[544,128]{1,0:T(8,128)S(1)}, u32[]{:S(2)}, u32[]{:S(2)}) collective-permute-start(f32[544,128]{1,0:T(8,128)S(1)} %get-tuple-element.9), channel_id=1, source_target_pairs={{0,1},{1,0},{2,3},{3,2},{4,5},{5,4},{6,7},{7,6},{8,9},{9,8},{10,11... | collective-permute-start | bytes 835592 | tf_op jit(solution)/shard_map/ppermute | solution.py:167
  115.4 1.2 collective-permute-done
  116.6 20.2 %all_to_all.21 = f32[32,1,2176]{2,1,0:T(1,128)S(1)} all-to-all(f32[32,1,2176]{2,1,0:T(1,128)S(1)} %bitcast.6), channel_id=1, replica_groups=mesh['x'=4,'y'=8,'z'=8,'core'=2] {'x','z'}, dimensions={0} | all-to-all | bytes 557056 | tf_op jit(solution)/shard_map/all_to_all | solution.py:163
  136.8 0.2 reduce_sum.18
  137.1 11.2 %all_to_all.22 = f32[8,1,2176]{2,1,0:T(1,128)S(1)} all-to-all(f32[8,1,2176]{2,1,0:T(1,128)S(1)} %broadcast_in_dim.4), channel_id=1, replica_groups=mesh['x'=4,'y'=8,'z'=8,'core'=2] {'y'}, dimensions={0} | all-to-all | bytes 139264 | tf_op jit(solution)/shard_map/all_to_all | solution.py:163
  148.3 0.1 reduce_sum.19
  148.4 0.1 broadcast_in_dim.5
  148.5 16.7 %all_to_all.23 = f32[32,1,2176]{2,1,0:T(1,128)S(1)} all-to-all(f32[32,1,2176]{2,1,0:T(1,128)S(1)} %broadcast_in_dim.5), channel_id=1, replica_groups=mesh['x'=4,'y'=8,'z'=8,'core'=2] {'x','z'}, dimensions={0} | all-to-all | bytes 557056 | tf_op jit(solution)/shard_map/all_to_all | solution.py:163
  165.2 6.9 %collective-permute-start.1 = (f32[544,128]{1,0:T(8,128)S(1)}, f32[544,128]{1,0:T(8,128)S(1)}, u32[]{:S(2)}, u32[]{:S(2)}) collective-permute-start(f32[544,128]{1,0:T(8,128)S(1)} %bitcast.3), channel_id=1, source_target_pairs={{0,1},{1,0},{2,3},{3,2},{4,5},{5,4},{6,7},{7,6},{8,9},{9,8},{10,11... | collective-permute-start | bytes 835592 | tf_op jit(solution)/shard_map/ppermute | solution.py:167
  172.1 1.2 collective-permute-done.1.other_ref
  173.2 0.0 copy-done
  173.2 10.8 %subspace_and_core.1 = bf16[128,4096]{1,0:T(8,128)(2,1)S(1)} custom-call(f32[544,128]{1,0:T(8,128)S(1)} %bitcast.4, f32[544,128]{1,0:T(8,128)S(1)} %collective-permute-done.1.other_ref, f32[512,128]{1,0:T(8,128)S(1)} %copy-done, bf16[64,2,16,2048]{3,2,1,0:T(8,128)(2,1)} %get-tuple-element.10.u_ref), custom_call_target="tpu_custom_call" | custom-call | tf_op jit(solution)/shard_map/subspace_and_core/pallas_call | solution.py:305
  184.0 1.6 reshape.25
  (2 shorter events, 0.1 us)
Async XLA Ops:
  106.6 66.6 %copy-start = (f32[512,128]{1,0:T(8,128)S(1)}, f32[512,128]{1,0:T(8,128)}, u32[]{:S(2)}) copy-start(f32[512,128]{1,0:T(8,128)} %start_ref.1) | copy-start | bytes 786436
  108.6 8.0 %collective-permute-start = (f32[544,128]{1,0:T(8,128)S(1)}, f32[544,128]{1,0:T(8,128)S(1)}, u32[]{:S(2)}, u32[]{:S(2)}) collective-permute-start(f32[544,128]{1,0:T(8,128)S(1)} %get-tuple-element.9), channel_id=1, source_target_pairs={{0,1},{1,0},{2,3},{3,2},{4,5},{5,4},{6,7},{7,6},{8,9},{9,8},{10,11... | collective-permute-start | bytes 835592 | tf_op jit(solution)/shard_map/ppermute | solution.py:167
  165.2 8.0 %collective-permute-start.1 = (f32[544,128]{1,0:T(8,128)S(1)}, f32[544,128]{1,0:T(8,128)S(1)}, u32[]{:S(2)}, u32[]{:S(2)}) collective-permute-start(f32[544,128]{1,0:T(8,128)S(1)} %bitcast.3), channel_id=1, source_target_pairs={{0,1},{1,0},{2,3},{3,2},{4,5},{5,4},{6,7},{7,6},{8,9},{9,8},{10,11... | collective-permute-start | bytes 835592 | tf_op jit(solution)/shard_map/ppermute | solution.py:167

commit v5 on v4

--- a/solution.py
+++ b/solution.py
@@ -7,11 +7,11 @@
 
 ITERS = 2
 SUB = 8
-BLOCK = 16
 TILE = 128
 TH_STEP = 16
+PH_STEP = 2048
 CELLS = 1024
-AHEAD = 4
+OUT_CELLS = 1024
 AXES = ("x", "y", "z", "core")
 SIZES = (4, 8, 8, 2)
 RAD = ("x", "y")
@@ -38,27 +38,24 @@
 
 
 def regroup_kernel(field_ref, out_ref, held_ref, moved_ref, sems, out_sems):
-    radii, th, _ = field_ref.shape
+    radii, th, ph = field_ref.shape
     rows = radii * TH_STEP
-    copies = []
-    for n in range(th // TH_STEP):
-        part = field_ref.at[:, pl.ds(TH_STEP * n, TH_STEP)]
+    places = [(t, c) for t in range(0, th, TH_STEP) for c in range(0, ph, PH_STEP)]
+    copies, results = [], []
+    for n, (t, c) in enumerate(places):
+        part = field_ref.at[:, pl.ds(t, TH_STEP), pl.ds(c, PH_STEP)]
         copies.append(pltpu.make_async_copy(part, held_ref.at[n], sems.at[n]))
-    for copy in copies[:AHEAD]:
-        copy.start()
+        copies[-1].start()
     to = lax.broadcasted_iota(jnp.int32, (rows, rows), 0)
     source = lax.broadcasted_iota(jnp.int32, (rows, rows), 1)
     moved = jnp.where((to // radii == source % TH_STEP) & (to % radii == source // TH_STEP), 1.0, 0.0)
     moved = moved.astype(jnp.bfloat16)
-    results = []
-    for n, copy in enumerate(copies):
-        copy.wait()
-        for later in copies[n + AHEAD:n + AHEAD + 1]:
-            later.start()
-        x = held_ref[n].reshape(rows, held_ref.shape[-1])
+    for n, (t, c) in enumerate(places):
+        copies[n].wait()
+        x = held_ref[n].reshape(rows, PH_STEP)
         y = jnp.dot(moved, x, preferred_element_type=jnp.float32).astype(jnp.bfloat16)
-        moved_ref[n] = y.reshape(TH_STEP, radii, held_ref.shape[-1])
-        part = out_ref.at[pl.ds(TH_STEP * n, TH_STEP)]
+        moved_ref[n] = y.reshape(TH_STEP, radii, PH_STEP)
+        part = out_ref.at[pl.ds(t, TH_STEP), :, pl.ds(c, PH_STEP)]
         results.append(pltpu.make_async_copy(moved_ref.at[n], part, out_sems.at[n]))
         results[-1].start()
     for result in results:
@@ -67,15 +64,15 @@
 
 def by_colatitude(field):
     radii, th, ph = field.shape
-    parts = th // TH_STEP
+    parts = (th // TH_STEP) * (ph // PH_STEP)
     return pl.pallas_call(
         regroup_kernel,
         in_specs=[pl.BlockSpec(memory_space=pltpu.HBM)],
         out_specs=pl.BlockSpec(memory_space=pltpu.HBM),
         out_shape=jax.ShapeDtypeStruct((th, radii, ph), field.dtype),
         scratch_shapes=[
-            pltpu.VMEM((parts, radii, TH_STEP, ph), field.dtype),
-            pltpu.VMEM((parts, TH_STEP, radii, ph), field.dtype),
+            pltpu.VMEM((parts, radii, TH_STEP, PH_STEP), field.dtype),
+            pltpu.VMEM((parts, TH_STEP, radii, PH_STEP), field.dtype),
             pltpu.SemaphoreType.DMA((parts,)),
             pltpu.SemaphoreType.DMA((parts,)),
         ],
@@ -198,6 +195,7 @@
 
 def inverse_lower(inner):
     n = inner.shape[0]
+    parts = n // SUB
     row = lax.broadcasted_iota(jnp.int32, (SUB, n), 0)
     col = lax.broadcasted_iota(jnp.int32, (SUB, n), 1)
 
@@ -207,58 +205,47 @@
     def pick(x, r):
         return jnp.broadcast_to(x[r:r + 1], (SUB, n))
 
-    def panels(x, count):
-        return [x[SUB * q:SUB * (q + 1)] for q in range(count)]
-
+    rows = [inner[SUB * q:SUB * (q + 1)] for q in range(parts)]
+    own = [spread(rows[0], j) for j in range(SUB)]
     done = []
-    left_rest, right_rest = inner, jnp.zeros_like(inner)
-    for start in range(0, n, BLOCK):
-        count = BLOCK // SUB
-        left = panels(left_rest, count)
-        right = [x + jnp.where(col == row + start + SUB * q, 1.0, 0.0) for q, x in enumerate(panels(right_rest, count))]
-        own = [spread(left[0], start + j) for j in range(SUB)]
-        scales, roots = [], []
-        for p in range(count):
-            at = start + SUB * p
-            more = p + 1 < count
+    for p in range(parts):
+        at = SUB * p
+        more = p + 1 < parts
+        inside = (col >= at) & (col < at + SUB)
+        if more:
+            below = [spread(rows[p + 1], at + j) for j in range(SUB)]
+            after = [spread(rows[p + 1], at + SUB + j) for j in range(SUB)]
+            rows[p + 1] = jnp.where(inside, 0.0, rows[p + 1])
+        rows[p] = jnp.where(inside, jnp.where(col == row + at, 1.0, 0.0), rows[p])
+        scale = jnp.ones((SUB, n), jnp.float32)
+        pivots = jnp.ones((SUB, n), jnp.float32)
+        for j in range(SUB):
+            pivot = pick(own[j], j)
+            inv = 1.0 / pivot
+            pivots = jnp.where(row == j, pivot, pivots)
+            scale = jnp.where(row == j, inv, scale)
+            lead_row = pick(rows[p], j)
+            lead = {c: pick(own[c], j) for c in range(j + 1, SUB)}
+            times = jnp.where(row > j, own[j], 0.0) * inv
+            for c in range(j + 1, SUB):
+                own[c] = own[c] - times * lead[c]
+            rows[p] = rows[p] - times * lead_row
             if more:
-                below = [spread(left[p + 1], at + j) for j in range(SUB)]
-                after = [spread(left[p + 1], at + SUB + j) for j in range(SUB)]
-            scale = jnp.ones((SUB, n), jnp.float32)
-            pivots = jnp.ones((SUB, n), jnp.float32)
-            for j in range(SUB):
-                pivot = pick(own[j], j)
-                inv = 1.0 / pivot
-                pivots = jnp.where(row == j, pivot, pivots)
-                scale = jnp.where(row == j, inv, scale)
-                lead_left, lead_right = pick(left[p], j), pick(right[p], j)
-                lead = {c: pick(own[c], j) for c in range(j + 1, SUB)}
-                times = jnp.where(row > j, own[j], 0.0) * inv
+                times = below[j] * inv
+                for c in range(SUB):
+                    after[c] = after[c] - times * pick(below[j], c)
                 for c in range(j + 1, SUB):
-                    own[c] = own[c] - times * lead[c]
-                left[p] = left[p] - times * lead_left
-                right[p] = right[p] - times * lead_right
-                if more:
-                    times = below[j] * inv
-                    for c in range(SUB):
-                        after[c] = after[c] - times * pick(below[j], c)
-                    for c in range(j + 1, SUB):
-                        below[c] = below[c] - times * lead[c]
-                    left[p + 1] = left[p + 1] - times * lead_left
-                    right[p + 1] = right[p + 1] - times * lead_right
-            scales.append(scale)
-            roots.append(jnp.sqrt(pivots))
-            if more:
-                own = after
-        left_block = jnp.concatenate(left, axis=0)
-        right_block = jnp.concatenate(right, axis=0)
-        done.append(right_block / jnp.concatenate(roots, axis=0))
-        if start + BLOCK < n:
-            scaled = left_block * jnp.concatenate(scales, axis=0)
-            change = outer(scaled, jnp.concatenate([left_block, right_block], axis=1))[start + BLOCK:]
-            left_rest = left_rest[BLOCK:] - change[:, :n]
-            right_rest = right_rest[BLOCK:] - change[:, n:]
-    return jnp.concatenate(done, axis=0)
+                    below[c] = below[c] - times * lead[c]
+                rows[p + 1] = rows[p + 1] - times * lead_row
+        done.append(rows[p] / jnp.sqrt(pivots))
+        if p + 2 < parts:
+            change = outer(rows[p] * scale, rows[p])
+            for q in range(p + 2, parts):
+                rows[q] = jnp.where(inside, 0.0, rows[q]) - change[SUB * q:SUB * (q + 1)]
+        if more:
+            own = after
+    lower = lax.broadcasted_iota(jnp.int32, (n, n), 0) >= lax.broadcasted_iota(jnp.int32, (n, n), 1)
+    return jnp.where(lower, jnp.concatenate(done, axis=0), 0.0)
 
 
 def exact(a, b, dims):
@@ -268,7 +255,9 @@
     )
 
 
-def core_kernel(mine_ref, other_ref, start_ref, u_ref, out_ref, gram_ref, basis_ref, held_ref, sem):
+def core_kernel(
+    mine_ref, other_ref, start_ref, u_ref, out_ref, gram_ref, basis_ref, held_ref, core_part_ref, sem, out_sems
+):
     copy = pltpu.make_async_copy(u_ref.at[pl.ds(0, held_ref.shape[0])], held_ref, sem)
     copy.start()
     core = lax.axis_index("core")
@@ -289,12 +278,17 @@
     narrow = basis_ref[...].astype(jnp.bfloat16)
     copy.wait()
     src, th, radii, ph = held_ref.shape
-    cells = 512
-    for t in range(th):
-        for c in range(ph // cells):
-            u = held_ref[:, t, :, cells * c:cells * (c + 1)].reshape(src * radii, cells)
-            core = jnp.dot(narrow, u, preferred_element_type=jnp.float32)
-            out_ref[:, t * ph + cells * c:t * ph + cells * (c + 1)] = core.astype(jnp.bfloat16)
+    results = []
+    for c in range(ph // OUT_CELLS):
+        cells = slice(OUT_CELLS * c, OUT_CELLS * (c + 1))
+        for t in range(th):
+            u = held_ref[:, t, :, cells].reshape(src * radii, OUT_CELLS)
+            core_part_ref[:, t, cells] = jnp.dot(narrow, u, preferred_element_type=jnp.float32).astype(jnp.bfloat16)
+        part = pl.ds(OUT_CELLS * c, OUT_CELLS)
+        results.append(pltpu.make_async_copy(core_part_ref.at[:, :, part], out_ref.at[:, :, part], out_sems.at[c]))
+        results[-1].start()
+    for result in results:
+        result.wait()
 
 
 def core_of(mine, other, start, held):
@@ -305,13 +299,15 @@
     return pl.pallas_call(
         core_kernel,
         in_specs=[vmem] * 3 + [pl.BlockSpec(memory_space=pltpu.HBM)],
-        out_specs=vmem,
-        out_shape=jax.ShapeDtypeStruct((rank, th * ph), jnp.bfloat16),
+        out_specs=pl.BlockSpec(memory_space=pltpu.HBM),
+        out_shape=jax.ShapeDtypeStruct((rank, th, ph), jnp.bfloat16),
         scratch_shapes=[
             pltpu.VMEM((order, order), jnp.float32),
             pltpu.VMEM((rank, order), jnp.float32),
             pltpu.VMEM((src, th, radii, ph), jnp.bfloat16),
+            pltpu.VMEM((rank, th, ph), jnp.bfloat16),
             pltpu.SemaphoreType.DMA,
+            pltpu.SemaphoreType.DMA((ph // OUT_CELLS,)),
         ],
         compiler_params=pltpu.CompilerParams(vmem_limit_bytes=VMEM_LIMIT),
         name="subspace_and_core",
@@ -325,8 +321,7 @@
     regrouped = swap(sent, RAD)
     keep, send, held = partial_gram(regrouped)
     mine, other = sum_everywhere(keep, send)
-    core = core_of(mine, other, start, held)
-    return core.reshape(start.shape[1], th // owners, ph)
+    return core_of(mine, other, start, held)
 
 
 def solution(mesh):

time: 186 us -> 185 us (level)
  no operation moved by 1% of the time
where the time goes in v5:
time: 185 us; the launch traced here: 184 us
  blocking collectives  151 us (82%)
  Pallas kernels  17.1 us (9%)
  starting transfers between devices  13.7 us (7%)
  waiting for transfers between devices  2.33 us (1%)
    all_to_all x4, blocking collectives, swap(): return lax.all_to_all(x, names, split_axis=0, concat_axis=0, tiled=True)  151 us
    ppermute x2, starting transfers between devices, swap_core(): return lax.ppermute(x, 'core', [(0, 1), (1, 0)])  13.7 us
    pallas_call x1, Pallas kernels, core_of(): pl.pallas_call(core_kernel, in_specs=[vmem] * 3 + [pl.BlockSpec(memory_sp...  11.1 us
    pallas_call x1, Pallas kernels, by_colatitude(): pl.pallas_call(regroup_kernel, in_specs=[pl.BlockSpec(memory_space=pltpu....  4.05 us
  transfers between devices with their start and end apart: 2, of which 2 were waited for; matrix products, arithmetic and copies ran while one was open for 0% of the time, Pallas kernels for 0%

profile of v5, /device:TPU:1, one launch (start us, length us, event | category | flops | bytes accessed | tf_op | source)
XLA Modules:
  0.0 184.3 jit_solution(15744608458956500384)
XLA Ops:
  0.0 4.1 %by_colatitude.1 = bf16[64,16,2048]{2,1,0:T(8,128)(2,1)} custom-call(bf16[16,64,2048]{2,1,0:T(8,128)(2,1)} %field_ref.1), custom_call_target="tpu_custom_call" | custom-call | tf_op jit(solution)/shard_map/by_colatitude/pallas_call | solution.py:68
  4.1 102.6 %all_to_all.20.u_ref = bf16[32,2,16,2048]{3,2,1,0:T(8,128)(2,1)S(1)} all-to-all(bf16[32,2,16,2048]{3,2,1,0:T(8,128)(2,1)} %bitcast.5), channel_id=1, replica_groups=mesh['x'=4,'y'=8,'z'=8,'core'=2] {'x','y'}, dimensions={0} | all-to-all | bytes 8388608 | tf_op jit(solution)/shard_map/all_to_all | solution.py:160
  106.6 0.0 copy-start
  106.6 1.9 %gram.1 = (f32[544,128]{1,0:T(8,128)S(1)}, f32[544,128]{1,0:T(8,128)S(1)}, bf16[64,2,16,2048]{3,2,1,0:T(8,128)(2,1)}) custom-call(bf16[32,2,16,2048]{3,2,1,0:T(8,128)(2,1)S(1)} %all_to_all.20.u_ref), custom_call_target="tpu_custom_call" | custom-call | tf_op jit(solution)/shard_map/gram/pallas_call | solution.py:130
  108.6 6.9 %collective-permute-start = (f32[544,128]{1,0:T(8,128)S(1)}, f32[544,128]{1,0:T(8,128)S(1)}, u32[]{:S(2)}, u32[]{:S(2)}) collective-permute-start(f32[544,128]{1,0:T(8,128)S(1)} %get-tuple-element.9), channel_id=1, source_target_pairs={{0,1},{1,0},{2,3},{3,2},{4,5},{5,4},{6,7},{7,6},{8,9},{9,8},{10,11... | collective-permute-start | bytes 835592 | tf_op jit(solution)/shard_map/ppermute | solution.py:164
  115.4 1.2 collective-permute-done
  116.6 20.2 %all_to_all.21 = f32[32,1,2176]{2,1,0:T(1,128)S(1)} all-to-all(f32[32,1,2176]{2,1,0:T(1,128)S(1)} %bitcast.6), channel_id=1, replica_groups=mesh['x'=4,'y'=8,'z'=8,'core'=2] {'x','z'}, dimensions={0} | all-to-all | bytes 557056 | tf_op jit(solution)/shard_map/all_to_all | solution.py:160
  136.8 0.2 reduce_sum.18
  137.1 11.2 %all_to_all.22 = f32[8,1,2176]{2,1,0:T(1,128)S(1)} all-to-all(f32[8,1,2176]{2,1,0:T(1,128)S(1)} %broadcast_in_dim.4), channel_id=1, replica_groups=mesh['x'=4,'y'=8,'z'=8,'core'=2] {'y'}, dimensions={0} | all-to-all | bytes 139264 | tf_op jit(solution)/shard_map/all_to_all | solution.py:160
  148.3 0.1 reduce_sum.19
  148.4 0.1 broadcast_in_dim.5
  148.5 16.7 %all_to_all.23 = f32[32,1,2176]{2,1,0:T(1,128)S(1)} all-to-all(f32[32,1,2176]{2,1,0:T(1,128)S(1)} %broadcast_in_dim.5), channel_id=1, replica_groups=mesh['x'=4,'y'=8,'z'=8,'core'=2] {'x','z'}, dimensions={0} | all-to-all | bytes 557056 | tf_op jit(solution)/shard_map/all_to_all | solution.py:160
  165.2 6.9 %collective-permute-start.1 = (f32[544,128]{1,0:T(8,128)S(1)}, f32[544,128]{1,0:T(8,128)S(1)}, u32[]{:S(2)}, u32[]{:S(2)}) collective-permute-start(f32[544,128]{1,0:T(8,128)S(1)} %bitcast.3), channel_id=1, source_target_pairs={{0,1},{1,0},{2,3},{3,2},{4,5},{5,4},{6,7},{7,6},{8,9},{9,8},{10,11... | collective-permute-start | bytes 835592 | tf_op jit(solution)/shard_map/ppermute | solution.py:164
  172.1 1.2 collective-permute-done.1.other_ref
  173.2 0.0 copy-done
  173.2 11.1 %subspace_and_core.1 = bf16[128,2,2048]{2,1,0:T(2,128)(2,1)} custom-call(f32[544,128]{1,0:T(8,128)S(1)} %bitcast.4, f32[544,128]{1,0:T(8,128)S(1)} %collective-permute-done.1.other_ref, f32[512,128]{1,0:T(8,128)S(1)} %copy-done, bf16[64,2,16,2048]{3,2,1,0:T(8,128)(2,1)} %get-tuple-element.10.u_ref), custom_call_target="tpu_custom_call" | custom-call | tf_op jit(solution)/shard_map/subspace_and_core/pallas_call | solution.py:299
  (2 shorter events, 0.1 us)
Async XLA Ops:
  106.6 66.6 %copy-start = (f32[512,128]{1,0:T(8,128)S(1)}, f32[512,128]{1,0:T(8,128)}, u32[]{:S(2)}) copy-start(f32[512,128]{1,0:T(8,128)} %start_ref.1) | copy-start | bytes 786436
  108.6 8.0 %collective-permute-start = (f32[544,128]{1,0:T(8,128)S(1)}, f32[544,128]{1,0:T(8,128)S(1)}, u32[]{:S(2)}, u32[]{:S(2)}) collective-permute-start(f32[544,128]{1,0:T(8,128)S(1)} %get-tuple-element.9), channel_id=1, source_target_pairs={{0,1},{1,0},{2,3},{3,2},{4,5},{5,4},{6,7},{7,6},{8,9},{9,8},{10,11... | collective-permute-start | bytes 835592 | tf_op jit(solution)/shard_map/ppermute | solution.py:164
  165.2 8.0 %collective-permute-start.1 = (f32[544,128]{1,0:T(8,128)S(1)}, f32[544,128]{1,0:T(8,128)S(1)}, u32[]{:S(2)}, u32[]{:S(2)}) collective-permute-start(f32[544,128]{1,0:T(8,128)S(1)} %bitcast.3), channel_id=1, source_target_pairs={{0,1},{1,0},{2,3},{3,2},{4,5},{5,4},{6,7},{7,6},{8,9},{9,8},{10,11... | collective-permute-start | bytes 835592 | tf_op jit(solution)/shard_map/ppermute | solution.py:164

commit v6 on v5

--- a/solution.py
+++ b/solution.py
@@ -7,9 +7,9 @@
 
 ITERS = 2
 SUB = 8
+LOOK = 3
 TILE = 128
 TH_STEP = 16
-PH_STEP = 2048
 CELLS = 1024
 OUT_CELLS = 1024
 AXES = ("x", "y", "z", "core")
@@ -19,6 +19,7 @@
 MID = ("y",)
 VMEM_LIMIT = 52 * 2**20
 GRAM_LIMIT = 46 * 2**20
+REGROUP_LIMIT = 48 * 2**20
 HELD_ROOM = 2
 
 
@@ -37,46 +38,35 @@
     return (lax.broadcasted_iota(jnp.int32, (TILE, TILE), d) for d in (0, 1))
 
 
-def regroup_kernel(field_ref, out_ref, held_ref, moved_ref, sems, out_sems):
+def regroup_kernel(field_ref, out_ref, held_ref, sems):
     radii, th, ph = field_ref.shape
     rows = radii * TH_STEP
-    places = [(t, c) for t in range(0, th, TH_STEP) for c in range(0, ph, PH_STEP)]
-    copies, results = [], []
-    for n, (t, c) in enumerate(places):
-        part = field_ref.at[:, pl.ds(t, TH_STEP), pl.ds(c, PH_STEP)]
+    copies = []
+    for n in range(th // TH_STEP):
+        part = field_ref.at[:, pl.ds(TH_STEP * n, TH_STEP)]
         copies.append(pltpu.make_async_copy(part, held_ref.at[n], sems.at[n]))
         copies[-1].start()
     to = lax.broadcasted_iota(jnp.int32, (rows, rows), 0)
     source = lax.broadcasted_iota(jnp.int32, (rows, rows), 1)
     moved = jnp.where((to // radii == source % TH_STEP) & (to % radii == source // TH_STEP), 1.0, 0.0)
     moved = moved.astype(jnp.bfloat16)
-    for n, (t, c) in enumerate(places):
-        copies[n].wait()
-        x = held_ref[n].reshape(rows, PH_STEP)
+    for n, copy in enumerate(copies):
+        copy.wait()
+        x = held_ref[n].reshape(rows, ph)
         y = jnp.dot(moved, x, preferred_element_type=jnp.float32).astype(jnp.bfloat16)
-        moved_ref[n] = y.reshape(TH_STEP, radii, PH_STEP)
-        part = out_ref.at[pl.ds(t, TH_STEP), :, pl.ds(c, PH_STEP)]
-        results.append(pltpu.make_async_copy(moved_ref.at[n], part, out_sems.at[n]))
-        results[-1].start()
-    for result in results:
-        result.wait()
+        out_ref[TH_STEP * n:TH_STEP * (n + 1)] = y.reshape(TH_STEP, radii, ph)
 
 
 def by_colatitude(field):
     radii, th, ph = field.shape
-    parts = (th // TH_STEP) * (ph // PH_STEP)
+    parts = th // TH_STEP
     return pl.pallas_call(
         regroup_kernel,
         in_specs=[pl.BlockSpec(memory_space=pltpu.HBM)],
-        out_specs=pl.BlockSpec(memory_space=pltpu.HBM),
+        out_specs=pl.BlockSpec(memory_space=pltpu.VMEM),
         out_shape=jax.ShapeDtypeStruct((th, radii, ph), field.dtype),
-        scratch_shapes=[
-            pltpu.VMEM((parts, radii, TH_STEP, PH_STEP), field.dtype),
-            pltpu.VMEM((parts, TH_STEP, radii, PH_STEP), field.dtype),
-            pltpu.SemaphoreType.DMA((parts,)),
-            pltpu.SemaphoreType.DMA((parts,)),
-        ],
-        compiler_params=pltpu.CompilerParams(vmem_limit_bytes=VMEM_LIMIT),
+        scratch_shapes=[pltpu.VMEM((parts, radii, TH_STEP, ph), field.dtype), pltpu.SemaphoreType.DMA((parts,))],
+        compiler_params=pltpu.CompilerParams(vmem_limit_bytes=REGROUP_LIMIT),
         name="by_colatitude",
     )(field)
 
@@ -210,12 +200,13 @@
     done = []
     for p in range(parts):
         at = SUB * p
-        more = p + 1 < parts
+        near = range(p + 1, min(parts, p + 1 + LOOK))
         inside = (col >= at) & (col < at + SUB)
-        if more:
-            below = [spread(rows[p + 1], at + j) for j in range(SUB)]
+        below = {q: [spread(rows[q], at + j) for j in range(SUB)] for q in near}
+        if near:
             after = [spread(rows[p + 1], at + SUB + j) for j in range(SUB)]
-            rows[p + 1] = jnp.where(inside, 0.0, rows[p + 1])
+        for q in near:
+            rows[q] = jnp.where(inside, 0.0, rows[q])
         rows[p] = jnp.where(inside, jnp.where(col == row + at, 1.0, 0.0), rows[p])
         scale = jnp.ones((SUB, n), jnp.float32)
         pivots = jnp.ones((SUB, n), jnp.float32)
@@ -230,19 +221,20 @@
             for c in range(j + 1, SUB):
                 own[c] = own[c] - times * lead[c]
             rows[p] = rows[p] - times * lead_row
-            if more:
-                times = below[j] * inv
-                for c in range(SUB):
-                    after[c] = after[c] - times * pick(below[j], c)
+            for q in near:
+                times = below[q][j] * inv
+                if q == p + 1:
+                    for c in range(SUB):
+                        after[c] = after[c] - times * pick(below[q][j], c)
                 for c in range(j + 1, SUB):
-                    below[c] = below[c] - times * lead[c]
-                rows[p + 1] = rows[p + 1] - times * lead_row
+                    below[q][c] = below[q][c] - times * lead[c]
+                rows[q] = rows[q] - times * lead_row
         done.append(rows[p] / jnp.sqrt(pivots))
-        if p + 2 < parts:
+        if p + 1 + LOOK < parts:
             change = outer(rows[p] * scale, rows[p])
-            for q in range(p + 2, parts):
+            for q in range(p + 1 + LOOK, parts):
                 rows[q] = jnp.where(inside, 0.0, rows[q]) - change[SUB * q:SUB * (q + 1)]
-        if more:
+        if near:
             own = after
     lower = lax.broadcasted_iota(jnp.int32, (n, n), 0) >= lax.broadcasted_iota(jnp.int32, (n, n), 1)
     return jnp.where(lower, jnp.concatenate(done, axis=0), 0.0)

time: 185 us -> 182 us (0.984)
  Pallas kernels: 17.1 us -> 15 us
where the time goes in v6:
time: 182 us
  blocking collectives  150 us (82%)
  Pallas kernels  15 us (8%)
  starting transfers between devices  13.7 us (8%)
  waiting for transfers between devices  2.33 us (1%)
    all_to_all x4, blocking collectives, swap(): return lax.all_to_all(x, names, split_axis=0, concat_axis=0, tiled=True)  150 us
    ppermute x2, starting transfers between devices, swap_core(): return lax.ppermute(x, 'core', [(0, 1), (1, 0)])  13.7 us
    pallas_call x1, Pallas kernels, core_of(): pl.pallas_call(core_kernel, in_specs=[vmem] * 3 + [pl.BlockSpec(memory_sp...  10.1 us
  transfers between devices with their start and end apart: 2, of which 2 were waited for; matrix products, arithmetic and copies ran while one was open for 0% of the time, Pallas kernels for 0%

profile of v6, /device:TPU:1, one launch (start us, length us, event | category | flops | bytes accessed | tf_op | source)
XLA Modules:
  0.0 182.1 jit_solution(14919403673249466714)
XLA Ops:
  0.0 3.0 %by_colatitude.1 = bf16[64,16,2048]{2,1,0:T(8,128)(2,1)S(1)} custom-call(bf16[16,64,2048]{2,1,0:T(8,128)(2,1)} %field_ref.1), custom_call_target="tpu_custom_call" | custom-call | tf_op jit(solution)/shard_map/by_colatitude/pallas_call | solution.py:63
  3.0 102.3 %all_to_all.20.u_ref = bf16[32,2,16,2048]{3,2,1,0:T(8,128)(2,1)S(1)} all-to-all(bf16[32,2,16,2048]{3,2,1,0:T(8,128)(2,1)S(1)} %bitcast.3), channel_id=1, replica_groups=mesh['x'=4,'y'=8,'z'=8,'core'=2] {'x','y'}, dimensions={0} | all-to-all | bytes 8388608 | tf_op jit(solution)/shard_map/all_to_all | solution.py:150
  105.4 0.0 copy-start
  105.4 1.9 %gram.1 = (f32[544,128]{1,0:T(8,128)S(1)}, f32[544,128]{1,0:T(8,128)S(1)}, bf16[64,2,16,2048]{3,2,1,0:T(8,128)(2,1)}) custom-call(bf16[32,2,16,2048]{3,2,1,0:T(8,128)(2,1)S(1)} %all_to_all.20.u_ref), custom_call_target="tpu_custom_call" | custom-call | tf_op jit(solution)/shard_map/gram/pallas_call | solution.py:120
  107.3 6.9 %collective-permute-start = (f32[544,128]{1,0:T(8,128)S(1)}, f32[544,128]{1,0:T(8,128)S(1)}, u32[]{:S(2)}, u32[]{:S(2)}) collective-permute-start(f32[544,128]{1,0:T(8,128)S(1)} %get-tuple-element.9), channel_id=1, source_target_pairs={{0,1},{1,0},{2,3},{3,2},{4,5},{5,4},{6,7},{7,6},{8,9},{9,8},{10,11... | collective-permute-start | bytes 835592 | tf_op jit(solution)/shard_map/ppermute | solution.py:154
  114.2 1.2 collective-permute-done
  115.4 20.2 %all_to_all.21 = f32[32,1,2176]{2,1,0:T(1,128)S(1)} all-to-all(f32[32,1,2176]{2,1,0:T(1,128)S(1)} %bitcast.6), channel_id=1, replica_groups=mesh['x'=4,'y'=8,'z'=8,'core'=2] {'x','z'}, dimensions={0} | all-to-all | bytes 557056 | tf_op jit(solution)/shard_map/all_to_all | solution.py:150
  135.6 0.2 reduce_sum.18
  135.8 11.2 %all_to_all.22 = f32[8,1,2176]{2,1,0:T(1,128)S(1)} all-to-all(f32[8,1,2176]{2,1,0:T(1,128)S(1)} %broadcast_in_dim.4), channel_id=1, replica_groups=mesh['x'=4,'y'=8,'z'=8,'core'=2] {'y'}, dimensions={0} | all-to-all | bytes 139264 | tf_op jit(solution)/shard_map/all_to_all | solution.py:150
  147.1 0.1 reduce_sum.19
  147.1 0.1 broadcast_in_dim.5
  147.3 16.7 %all_to_all.23 = f32[32,1,2176]{2,1,0:T(1,128)S(1)} all-to-all(f32[32,1,2176]{2,1,0:T(1,128)S(1)} %broadcast_in_dim.5), channel_id=1, replica_groups=mesh['x'=4,'y'=8,'z'=8,'core'=2] {'x','z'}, dimensions={0} | all-to-all | bytes 557056 | tf_op jit(solution)/shard_map/all_to_all | solution.py:150
  164.0 6.9 %collective-permute-start.1 = (f32[544,128]{1,0:T(8,128)S(1)}, f32[544,128]{1,0:T(8,128)S(1)}, u32[]{:S(2)}, u32[]{:S(2)}) collective-permute-start(f32[544,128]{1,0:T(8,128)S(1)} %bitcast.4), channel_id=1, source_target_pairs={{0,1},{1,0},{2,3},{3,2},{4,5},{5,4},{6,7},{7,6},{8,9},{9,8},{10,11... | collective-permute-start | bytes 835592 | tf_op jit(solution)/shard_map/ppermute | solution.py:154
  170.8 1.2 collective-permute-done.1.other_ref
  172.0 0.0 copy-done
  172.0 10.1 %subspace_and_core.1 = bf16[128,2,2048]{2,1,0:T(2,128)(2,1)} custom-call(f32[544,128]{1,0:T(8,128)S(1)} %bitcast.5, f32[544,128]{1,0:T(8,128)S(1)} %collective-permute-done.1.other_ref, f32[512,128]{1,0:T(8,128)S(1)} %copy-done, bf16[64,2,16,2048]{3,2,1,0:T(8,128)(2,1)} %get-tuple-element.10.u_ref), custom_call_target="tpu_custom_call" | custom-call | tf_op jit(solution)/shard_map/subspace_and_core/pallas_call | solution.py:291
  (2 shorter events, 0.1 us)
Async XLA Ops:
  105.4 66.6 %copy-start = (f32[512,128]{1,0:T(8,128)S(1)}, f32[512,128]{1,0:T(8,128)}, u32[]{:S(2)}) copy-start(f32[512,128]{1,0:T(8,128)} %start_ref.1) | copy-start | bytes 786436
  107.3 8.0 %collective-permute-start = (f32[544,128]{1,0:T(8,128)S(1)}, f32[544,128]{1,0:T(8,128)S(1)}, u32[]{:S(2)}, u32[]{:S(2)}) collective-permute-start(f32[544,128]{1,0:T(8,128)S(1)} %get-tuple-element.9), channel_id=1, source_target_pairs={{0,1},{1,0},{2,3},{3,2},{4,5},{5,4},{6,7},{7,6},{8,9},{9,8},{10,11... | collective-permute-start | bytes 835592 | tf_op jit(solution)/shard_map/ppermute | solution.py:154
  164.0 8.0 %collective-permute-start.1 = (f32[544,128]{1,0:T(8,128)S(1)}, f32[544,128]{1,0:T(8,128)S(1)}, u32[]{:S(2)}, u32[]{:S(2)}) collective-permute-start(f32[544,128]{1,0:T(8,128)S(1)} %bitcast.4), channel_id=1, source_target_pairs={{0,1},{1,0},{2,3},{3,2},{4,5},{5,4},{6,7},{7,6},{8,9},{9,8},{10,11... | collective-permute-start | bytes 835592 | tf_op jit(solution)/shard_map/ppermute | solution.py:154

commit v7 on v6

--- a/solution.py
+++ b/solution.py
@@ -8,6 +8,7 @@
 ITERS = 2
 SUB = 8
 LOOK = 3
+CARRY = 2
 TILE = 128
 TH_STEP = 16
 CELLS = 1024
@@ -197,14 +198,16 @@
 
     rows = [inner[SUB * q:SUB * (q + 1)] for q in range(parts)]
     own = [spread(rows[0], j) for j in range(SUB)]
+    below = {}
     done = []
     for p in range(parts):
         at = SUB * p
         near = range(p + 1, min(parts, p + 1 + LOOK))
         inside = (col >= at) & (col < at + SUB)
-        below = {q: [spread(rows[q], at + j) for j in range(SUB)] for q in near}
-        if near:
-            after = [spread(rows[p + 1], at + SUB + j) for j in range(SUB)]
+        for q in near:
+            if q not in below:
+                below[q] = [spread(rows[q], at + j) for j in range(SUB)]
+        after = {q: [spread(rows[q], at + SUB + j) for j in range(SUB)] for q in near if q <= p + CARRY}
         for q in near:
             rows[q] = jnp.where(inside, 0.0, rows[q])
         rows[p] = jnp.where(inside, jnp.where(col == row + at, 1.0, 0.0), rows[p])
@@ -221,11 +224,12 @@
             for c in range(j + 1, SUB):
                 own[c] = own[c] - times * lead[c]
             rows[p] = rows[p] - times * lead_row
+            if near:
+                ahead = [pick(below[p + 1][j], c) for c in range(SUB)]
             for q in near:
                 times = below[q][j] * inv
-                if q == p + 1:
-                    for c in range(SUB):
-                        after[c] = after[c] - times * pick(below[q][j], c)
+                if q in after:
+                    after[q] = [x - times * y for x, y in zip(after[q], ahead)]
                 for c in range(j + 1, SUB):
                     below[q][c] = below[q][c] - times * lead[c]
                 rows[q] = rows[q] - times * lead_row
@@ -235,7 +239,8 @@
             for q in range(p + 1 + LOOK, parts):
                 rows[q] = jnp.where(inside, 0.0, rows[q]) - change[SUB * q:SUB * (q + 1)]
         if near:
-            own = after
+            own = after.pop(p + 1)
+            below = after
     lower = lax.broadcasted_iota(jnp.int32, (n, n), 0) >= lax.broadcasted_iota(jnp.int32, (n, n), 1)
     return jnp.where(lower, jnp.concatenate(done, axis=0), 0.0)
 

time: 182 us -> 182 us (level)
  no operation moved by 1% of the time
where the time goes in v7:
time: 182 us
  blocking collectives  150 us (82%)
  Pallas kernels  14.7 us (8%)
  starting transfers between devices  13.7 us (8%)
  waiting for transfers between devices  2.33 us (1%)
    all_to_all x4, blocking collectives, swap(): return lax.all_to_all(x, names, split_axis=0, concat_axis=0, tiled=True)  150 us
    ppermute x2, starting transfers between devices, swap_core(): return lax.ppermute(x, 'core', [(0, 1), (1, 0)])  13.7 us
    pallas_call x1, Pallas kernels, core_of(): pl.pallas_call(core_kernel, in_specs=[vmem] * 3 + [pl.BlockSpec(memory_sp...  9.72 us
  transfers between devices with their start and end apart: 2, of which 2 were waited for; matrix products, arithmetic and copies ran while one was open for 0% of the time, Pallas kernels for 0%

profile of v7, /device:TPU:1, one launch (start us, length us, event | category | flops | bytes accessed | tf_op | source)
XLA Modules:
  0.0 181.7 jit_solution(3379016348908206144)
XLA Ops:
  0.0 3.0 %by_colatitude.1 = bf16[64,16,2048]{2,1,0:T(8,128)(2,1)S(1)} custom-call(bf16[16,64,2048]{2,1,0:T(8,128)(2,1)} %field_ref.1), custom_call_target="tpu_custom_call" | custom-call | tf_op jit(solution)/shard_map/by_colatitude/pallas_call | solution.py:64
  3.0 102.3 %all_to_all.20.u_ref = bf16[32,2,16,2048]{3,2,1,0:T(8,128)(2,1)S(1)} all-to-all(bf16[32,2,16,2048]{3,2,1,0:T(8,128)(2,1)S(1)} %bitcast.3), channel_id=1, replica_groups=mesh['x'=4,'y'=8,'z'=8,'core'=2] {'x','y'}, dimensions={0} | all-to-all | bytes 8388608 | tf_op jit(solution)/shard_map/all_to_all | solution.py:151
  105.4 0.0 copy-start
  105.4 1.9 %gram.1 = (f32[544,128]{1,0:T(8,128)S(1)}, f32[544,128]{1,0:T(8,128)S(1)}, bf16[64,2,16,2048]{3,2,1,0:T(8,128)(2,1)}) custom-call(bf16[32,2,16,2048]{3,2,1,0:T(8,128)(2,1)S(1)} %all_to_all.20.u_ref), custom_call_target="tpu_custom_call" | custom-call | tf_op jit(solution)/shard_map/gram/pallas_call | solution.py:121
  107.3 6.9 %collective-permute-start = (f32[544,128]{1,0:T(8,128)S(1)}, f32[544,128]{1,0:T(8,128)S(1)}, u32[]{:S(2)}, u32[]{:S(2)}) collective-permute-start(f32[544,128]{1,0:T(8,128)S(1)} %get-tuple-element.9), channel_id=1, source_target_pairs={{0,1},{1,0},{2,3},{3,2},{4,5},{5,4},{6,7},{7,6},{8,9},{9,8},{10,11... | collective-permute-start | bytes 835592 | tf_op jit(solution)/shard_map/ppermute | solution.py:155
  114.2 1.2 collective-permute-done
  115.4 20.2 %all_to_all.21 = f32[32,1,2176]{2,1,0:T(1,128)S(1)} all-to-all(f32[32,1,2176]{2,1,0:T(1,128)S(1)} %bitcast.6), channel_id=1, replica_groups=mesh['x'=4,'y'=8,'z'=8,'core'=2] {'x','z'}, dimensions={0} | all-to-all | bytes 557056 | tf_op jit(solution)/shard_map/all_to_all | solution.py:151
  135.6 0.2 reduce_sum.18
  135.8 11.2 %all_to_all.22 = f32[8,1,2176]{2,1,0:T(1,128)S(1)} all-to-all(f32[8,1,2176]{2,1,0:T(1,128)S(1)} %broadcast_in_dim.4), channel_id=1, replica_groups=mesh['x'=4,'y'=8,'z'=8,'core'=2] {'y'}, dimensions={0} | all-to-all | bytes 139264 | tf_op jit(solution)/shard_map/all_to_all | solution.py:151
  147.1 0.1 reduce_sum.19
  147.1 0.1 broadcast_in_dim.5
  147.3 16.7 %all_to_all.23 = f32[32,1,2176]{2,1,0:T(1,128)S(1)} all-to-all(f32[32,1,2176]{2,1,0:T(1,128)S(1)} %broadcast_in_dim.5), channel_id=1, replica_groups=mesh['x'=4,'y'=8,'z'=8,'core'=2] {'x','z'}, dimensions={0} | all-to-all | bytes 557056 | tf_op jit(solution)/shard_map/all_to_all | solution.py:151
  164.0 6.9 %collective-permute-start.1 = (f32[544,128]{1,0:T(8,128)S(1)}, f32[544,128]{1,0:T(8,128)S(1)}, u32[]{:S(2)}, u32[]{:S(2)}) collective-permute-start(f32[544,128]{1,0:T(8,128)S(1)} %bitcast.4), channel_id=1, source_target_pairs={{0,1},{1,0},{2,3},{3,2},{4,5},{5,4},{6,7},{7,6},{8,9},{9,8},{10,11... | collective-permute-start | bytes 835592 | tf_op jit(solution)/shard_map/ppermute | solution.py:155
  170.8 1.2 collective-permute-done.1.other_ref
  172.0 0.0 copy-done
  172.0 9.7 %subspace_and_core.1 = bf16[128,2,2048]{2,1,0:T(2,128)(2,1)} custom-call(f32[544,128]{1,0:T(8,128)S(1)} %bitcast.5, f32[544,128]{1,0:T(8,128)S(1)} %collective-permute-done.1.other_ref, f32[512,128]{1,0:T(8,128)S(1)} %copy-done, bf16[64,2,16,2048]{3,2,1,0:T(8,128)(2,1)} %get-tuple-element.10.u_ref), custom_call_target="tpu_custom_call" | custom-call | tf_op jit(solution)/shard_map/subspace_and_core/pallas_call | solution.py:296
  (2 shorter events, 0.1 us)
Async XLA Ops:
  105.4 66.6 %copy-start = (f32[512,128]{1,0:T(8,128)S(1)}, f32[512,128]{1,0:T(8,128)}, u32[]{:S(2)}) copy-start(f32[512,128]{1,0:T(8,128)} %start_ref.1) | copy-start | bytes 786436
  107.3 8.0 %collective-permute-start = (f32[544,128]{1,0:T(8,128)S(1)}, f32[544,128]{1,0:T(8,128)S(1)}, u32[]{:S(2)}, u32[]{:S(2)}) collective-permute-start(f32[544,128]{1,0:T(8,128)S(1)} %get-tuple-element.9), channel_id=1, source_target_pairs={{0,1},{1,0},{2,3},{3,2},{4,5},{5,4},{6,7},{7,6},{8,9},{9,8},{10,11... | collective-permute-start | bytes 835592 | tf_op jit(solution)/shard_map/ppermute | solution.py:155
  164.0 8.0 %collective-permute-start.1 = (f32[544,128]{1,0:T(8,128)S(1)}, f32[544,128]{1,0:T(8,128)S(1)}, u32[]{:S(2)}, u32[]{:S(2)}) collective-permute-start(f32[544,128]{1,0:T(8,128)S(1)} %bitcast.4), channel_id=1, source_target_pairs={{0,1},{1,0},{2,3},{3,2},{4,5},{5,4},{6,7},{7,6},{8,9},{9,8},{10,11... | collective-permute-start | bytes 835592 | tf_op jit(solution)/shard_map/ppermute | solution.py:155
